TPU v7x, 32 devices: a whole 2x2x4 slice. The times are simulated.
32 devices in a mesh: rep: 4 (over y, x), fsdp: 8 (over z, core).
Axes of the slice: x: 2, y: 2, z: 4, core: 2. Of those that a mesh axis runs over, the one named last changes fastest.
Arguments:
- block_input: bfloat16 [4096, 4096], P(('rep', 'fsdp')), may hold values from -6 to 6
- ssd_input: bfloat16 [4096, 4096], P(('rep', 'fsdp')), may hold values from -6 to 6
- out_grad: bfloat16 [4096, 4096], P(('rep', 'fsdp')), may hold values from -0.29882812 to 0.29882812
- start_state: bfloat16 [32, 64, 4096], P(('rep', 'fsdp')), may hold values from -12 to 12
- step_bias: float32 [64], replicated, may hold values from -1 to 1
- decay_log: float32 [64], replicated, may hold values from -7 to -2.5
- local_params: float32 [4, 192, 4096], P('rep', 'fsdp'), may hold values from -0.09375 to 0.09375
- global_params: float32 [192, 4096], P('fsdp'), may hold values from -0.75 to 0.75
- momentum: float32 [192, 4096], P('fsdp'), may hold values from -3 to 3
Outputs:
- block_grad: bfloat16 [4096, 4096], P(('rep', 'fsdp'))
- new_params: float32 [192, 4096], P('fsdp')
- new_momentum: float32 [192, 4096], P('fsdp')
All inputs are finite; a program needn't handle non-finite values.
Results may differ from a plain program's by a relative error of at most 0.012.
Values may be sent and summed in bfloat16 or wider, within the bound.
No kernel may reach another device: no remote copies, remote signals or barrier semaphores. Data moves between devices by JAX's collectives and lax.ppermute only.
A program may use at most 64 MiB of HBM per device.

v0:
```python
import jax
import jax.numpy as jnp
from jax import lax
from jax.sharding import PartitionSpec as P

HEADS = 64
HEAD_DIM = 64
STATE = 64
BLOCK = 128


inner_rate = 0.002
outer_rate = 0.7
momentum_decay = 0.9


def contract_last(left, right):
    return lax.dot_general(
        left, right, (((1,), (1,)), ((), ())), preferred_element_type=jnp.float32
    )


def ssd_forward(projected, values, carried_in, step_bias, decay_log):
    key_side = projected[:, :STATE]
    query_side = projected[:, STATE : 2 * STATE]
    step_size = jax.nn.softplus(projected[:, 2 * STATE :] + step_bias)
    cumulative = jnp.cumsum(-step_size * jnp.exp(decay_log), axis=0)
    positions = jnp.arange(BLOCK)
    causal = positions[:, None] >= positions[None, :]
    spans = cumulative.T[:, :, None] - cumulative.T[:, None, :]
    decays = jnp.where(causal, jnp.exp(jnp.where(causal, spans, 0.0)), 0.0)
    scores = jnp.dot(query_side, key_side.T, precision=lax.Precision.HIGHEST)
    mixing = scores[None] * decays
    scaled = values.astype(jnp.float32).reshape(BLOCK, HEADS, HEAD_DIM) * step_size[:, :, None]
    within = jnp.einsum("hts,shp->thp", mixing, scaled, precision=lax.Precision.HIGHEST)
    state_f = carried_in.astype(jnp.float32).reshape(HEADS, HEAD_DIM, STATE)
    entering = jnp.einsum("tn,hpn->thp", query_side, state_f, precision=lax.Precision.HIGHEST)
    entering = entering * jnp.exp(cumulative)[:, :, None]
    return (within + entering).reshape(BLOCK, HEADS * HEAD_DIM)


def sequence_grads(projected, ssd_rows, cot_rows, states, step_bias, decay_log):
    blocks = projected.shape[0] // BLOCK

    def single(members):
        proj_one, values, cotangent, carried_in = members
        _, pullback = jax.vjp(
            lambda probe: ssd_forward(probe, values, carried_in, step_bias, decay_log), proj_one
        )
        return pullback(cotangent.astype(jnp.float32))[0]

    grads = lax.map(
        single,
        (
            projected.reshape(blocks, BLOCK, -1),
            ssd_rows.reshape(blocks, BLOCK, -1),
            cot_rows.reshape(blocks, BLOCK, -1),
            states,
        ),
    )
    return grads.reshape(blocks * BLOCK, -1)


def on_device(
    block_input,
    ssd_input,
    out_grad,
    start_state,
    step_bias,
    decay_log,
    local_params,
    global_params,
    momentum,
):
    local_rows = local_params[0]
    weights_shard = local_rows.astype(jnp.bfloat16)
    gathered = lax.all_gather(weights_shard, "fsdp", axis=0, tiled=True)
    projected = contract_last(block_input, gathered)
    proj_grad = sequence_grads(
        projected, ssd_input, out_grad, start_state, step_bias, decay_log
    ).astype(jnp.bfloat16)
    block_grad = jnp.dot(proj_grad, gathered, preferred_element_type=jnp.float32)
    block_grad = block_grad.astype(jnp.bfloat16)
    gradient = lax.psum_scatter(
        lax.dot_general(
            proj_grad, block_input, (((0,), (0,)), ((), ())), preferred_element_type=jnp.float32
        ),
        "fsdp",
        scatter_dimension=0,
        tiled=True,
    )
    pseudo = global_params - (local_rows - inner_rate * gradient)
    mean_pseudo = lax.psum(pseudo.astype(jnp.bfloat16), "rep").astype(jnp.float32) / lax.axis_size(
        "rep"
    )
    new_momentum = momentum_decay * momentum + mean_pseudo
    new_params = global_params - outer_rate * (mean_pseudo + momentum_decay * new_momentum)
    return (block_grad, new_params, new_momentum)


def solution(mesh):
    placed = (
        P(("rep", "fsdp"), None),
        P(("rep", "fsdp"), None),
        P(("rep", "fsdp"), None),
        P(("rep", "fsdp"), None, None),
        P(),
        P(),
        P("rep", "fsdp", None),
        P("fsdp", None),
        P("fsdp", None),
    )
    return jax.shard_map(
        on_device,
        mesh=mesh,
        in_specs=placed,
        out_specs=(P(("rep", "fsdp"), None), P("fsdp", None), P("fsdp", None)),
        check_vma=False,
    )
```

profile of v0, /device:TPU:0, one launch (start us, length us, event | category | flops | bytes accessed | tf_op | source)
XLA Modules:
  0.0 154.3 jit_solution(10583426775827272703)
XLA Ops:
  7.2 1.8 %bitcast_convert_fusion = bf16[24,4096]{1,0:T(8,128)(2,1)} fusion(f32[1,24,4096]{2,1,0:T(8,128)} %param.15), kind=kLoop, calls=%fused_computation.28 | loop fusion | flops 98304 | bytes 589824 | tf_op jit(solution)/shard_map/convert_element_type | solution.py:76
  9.0 0.0 reduce-scatter.2.cloned.1.call-start
  9.1 0.7 exp.27
  9.7 1.6 %copy.53 = bf16[128,4096]{0,1:T(8,128)(2,1)S(1)} copy(bf16[128,4096]{1,0:T(8,128)(2,1)} %param.11) | data formatting | bytes 2097152 | tf_op args[2]
  11.4 2.1 %reshape.66 = bf16[64,64,64]{2,1,0:T(8,128)(2,1)S(1)} reshape(bf16[1,64,4096]{2,1,0:T(8,128)(2,1)} %param.12) | data formatting | bytes 1048576 | tf_op jit(solution)/shard_map/while/body/eval_jaxpr/jvp()/reshape | solution.py:36
  13.4 2.6 %copy.48 = f32[128,4096]{0,1:T(8,128)} copy(bf16[128,4096]{1,0:T(8,128)(2,1)} %param.10) | data formatting | bytes 3145728 | tf_op jit(solution)/shard_map/while/body/eval_jaxpr/jvp()/convert_element_type | solution.py:34
  16.1 22.0 %all-gather.2.cloned.1.call-done = bf16[192,4096]{1,0:T(8,128)(2,1)} async-done(((bf16[24,4096]{1,0:T(8,128)(2,1)}), bf16[192,4096]{1,0:T(8,128)(2,1)}) %all-gather.2.cloned.1.call-update) | async-done | bytes 1572880 | tf_op jit(solution)/shard_map/all_gather | solution.py:77
  38.0 2.0 %fusion.36 = f32[128,192]{0,1:T(8,128)S(1)} fusion(bf16[128,4096]{1,0:T(8,128)(2,1)S(1)} %copy-done, bf16[192,4096]{1,0:T(8,128)(2,1)} %all-gather.2.cloned.1.call-done), kind=kOutput, calls=%fused_computation.56 | convolution fusion | flops 201326592 | bytes 2719744 | tf_op jit(solution)/shard_map/dot_general | solution.py:18
  40.0 0.3 fusion.28
  40.3 0.1 negate_multiply_fusion
  40.4 0.1 copy.50
  40.5 0.2 reduce_window_sum.24
  40.7 0.1 copy.56
  40.7 0.1 copy.51
  40.9 6.8 %fusion.10 = f32[128,64]{0,1:T(8,128)} fusion(f32[128,64,64]{0,2,1:T(8,128)} %bitcast.62, bf16[64,64,128]{2,1,0:T(8,128)(2,1)S(1)} %bitcast.58, f32[64,128]{1,0:T(8,128)S(1)} %copy.51, f32[128,128]{0,1:T(8,128)S(1)} %fusion.28, pred[128,128]{0,1:T(8,128)(4,1)S(1)} %iota_compare_fusion), kind=kOutput, calls=%fused_computation.15 | convolution fusion | flops 810541056 | bytes 3293184 | tf_op jit(solution)/shard_map/while/body/eval_jaxpr/transpose(jvp(hts,shp->thp))/dot_general | solution.py:35
  47.7 6.4 %fusion.9 = (f32[64,128]{1,0:T(8,128)S(1)}, f32[64,128]{1,0:T(8,128)S(1)}, f32[128,128]{0,1:T(8,128)S(1)}) fusion(f32[64,128]{1,0:T(8,128)S(1)} %copy.51, f32[128,128]{0,1:T(8,128)S(1)} %fusion.28, pred[128,128]{0,1:T(8,128)(4,1)S(1)} %iota_compare_fusion, bf16[64,64,128]{2,1,0:T(8,128)(2,1)S(1)} %bitcast.59, f32[128,64,64]{0,2,1:T(8,128)S(1)} %bitcast.63, ...), kind=kOutput, calls=%fused_computation.12 | convolution fusion | flops 817332224 | bytes 3424256 | tf_op jit(solution)/shard_map/while/body/eval_jaxpr/transpose(jvp(hts,shp->thp))/dot_general | solution.py:35
  54.0 0.2 fusion.30
  54.3 1.0 multiply_reduce_fusion
  55.3 0.1 copy.57
  55.4 1.1 reduce_window_sum.25
  56.5 0.1 copy.58
  56.6 0.2 bitcast_multiply_fusion.2
  56.8 1.4 convolution_bitcast_fusion
  58.2 0.2 convolution_add_fusion
  58.4 0.1 fusion.25
  58.5 2.2 %fusion.35 = f32[192,4096]{1,0:T(8,128)} fusion(bf16[128,4096]{1,0:T(8,128)(2,1)S(1)} %copy-done, f32[128,64]{0,1:T(8,128)S(1)} %fusion.30, f32[128,64]{0,1:T(8,128)S(1)} %convolution_add_fusion, f32[128,64]{0,1:T(8,128)S(1)} %fusion.25), kind=kOutput, calls=%fused_computation.55 | convolution fusion | flops 201400320 | bytes 4292608 | tf_op jit(solution)/shard_map/dot_general | solution.py:85
  60.8 0.0 all-reduce.5.cloned.1.call-start
  60.8 40.0 %reduce-scatter.2.cloned.1.call-done = f32[24,4096]{1,0:T(8,128)} async-done(((f32[192,4096]{1,0:T(8,128)}), f32[24,4096]{1,0:T(8,128)}) %reduce-scatter.2.cloned.1.call-update) | async-done | bytes 393232 | tf_op jit(solution)/shard_map/reduce_scatter | solution.py:84
  100.8 1.7 %fusion.22 = bf16[24,4096]{1,0:T(8,128)(2,1)} fusion(f32[24,4096]{1,0:T(8,128)S(1)} %copy-done.3, f32[1,24,4096]{2,1,0:T(8,128)S(1)} %copy-done.4, f32[24,4096]{1,0:T(8,128)} %reduce-scatter.2.cloned.1.call-done), kind=kLoop, calls=%fused_computation.30 | loop fusion | flops 393216 | bytes 1376256 | tf_op jit(solution)/shard_map/convert_element_type | solution.py:93
  102.5 1.5 convolution_convert_fusion
  104.0 41.8 %all-reduce.5.cloned.1.call-done = bf16[24,4096]{1,0:T(8,128)(2,1)} async-done(((bf16[24,4096]{1,0:T(8,128)(2,1)}), bf16[24,4096]{1,0:T(8,128)(2,1)}) %all-reduce.5.cloned.1.call-update) | async-done | bytes 196624 | tf_op jit(solution)/shard_map/psum | solution.py:93
  145.8 1.9 %multiply_subtract_fusion = (f32[24,4096]{1,0:T(8,128)}, f32[24,4096]{1,0:T(8,128)}) fusion(f32[24,4096]{1,0:T(8,128)S(1)} %copy-done.3, bf16[24,4096]{1,0:T(8,128)(2,1)} %all-reduce.5.cloned.1.call-done, f32[24,4096]{1,0:T(8,128)S(1)} %copy-done.5), kind=kLoop, calls=%fused_computation.31 | loop fusion | flops 786432 | bytes 1769472 | tf_op jit(solution)/shard_map/sub | solution.py:97
  (22 shorter events, 0.2 us)
Async XLA Ops:
  7.2 30.9 %copy-start = (bf16[128,4096]{1,0:T(8,128)(2,1)S(1)}, bf16[128,4096]{1,0:T(8,128)(2,1)}, u32[]{:S(2)}) copy-start(bf16[128,4096]{1,0:T(8,128)(2,1)} %param.9) | copy-start | bytes 3145732
  7.2 30.8 %all-gather.2.cloned.1.call-start = ((), (), s32[]{:S(2)}) async-start(), calls=%async_computation.1 | async-start | bytes 1769472 | tf_op jit(solution)/shard_map/all_gather | solution.py:77
  9.0 91.7 %reduce-scatter.2.cloned.1.call-start = ((), (), s32[]{:S(2)}) async-start(), calls=%async_computation.2 | async-start | bytes 3538944 | tf_op jit(solution)/shard_map/reduce_scatter | solution.py:84
  16.0 24.3 %copy-start.7 = (f32[64]{0:T(128)S(1)}, f32[64]{0:T(128)}, u32[]{:S(2)}) copy-start(f32[64]{0:T(128)} %param.13) | copy-start | bytes 772
  40.8 6.9 %copy-start.2 = (f32[128,4096]{0,1:T(8,128)S(1)}, f32[128,4096]{0,1:T(8,128)}, u32[]{:S(2)}) copy-start(f32[128,4096]{0,1:T(8,128)} %copy.48) | copy-start | bytes 6291460
  56.7 1.6 %copy-start.6 = (f32[128,64]{0,1:T(8,128)S(1)}, f32[128,64]{0,1:T(8,128)}, u32[]{:S(2)}) copy-start(f32[128,64]{0,1:T(8,128)} %fusion.10) | copy-start | bytes 98308
  60.7 40.0 %copy-start.3 = (f32[24,4096]{1,0:T(8,128)S(1)}, f32[24,4096]{1,0:T(8,128)}, u32[]{:S(2)}) copy-start(f32[24,4096]{1,0:T(8,128)} %param.16) | copy-start | bytes 1179652
  60.7 40.0 %copy-start.4 = (f32[1,24,4096]{2,1,0:T(8,128)S(1)}, f32[1,24,4096]{2,1,0:T(8,128)}, u32[]{:S(2)}) copy-start(f32[1,24,4096]{2,1,0:T(8,128)} %param.15) | copy-start | bytes 1179652
  60.7 41.8 %copy-start.1 = (bf16[192,4096]{1,0:T(8,128)(2,1)S(1)}, bf16[192,4096]{1,0:T(8,128)(2,1)}, u32[]{:S(2)}) copy-start(bf16[192,4096]{1,0:T(8,128)(2,1)} %all-gather.2.cloned.1.call-done) | copy-start | bytes 4718596
  60.8 85.1 %all-reduce.5.cloned.1.call-start = ((), (), s32[]{:S(2)}) async-start(), calls=%async_computation.3 | async-start | bytes 393216 | tf_op jit(solution)/shard_map/psum | solution.py:93
  102.5 43.3 %copy-start.5 = (f32[24,4096]{1,0:T(8,128)S(1)}, f32[24,4096]{1,0:T(8,128)}, u32[]{:S(2)}) copy-start(f32[24,4096]{1,0:T(8,128)} %param.17) | copy-start | bytes 1179652
Sparse Core Ops, SparseCore 0:
  10.2 27.7 all-gather.1
  60.9 39.8 reduce-scatter.1
  104.2 41.5 all-reduce.4
where the time goes:
time: 155 us; the launch traced here: 154 us
  waiting for transfers between devices  104 us (67%)
  matrix products  22 us (14%)
  between operations  13.9 us (9%)
  local copies, waits for them, and re-layouts  7.39 us (5%)
  other arithmetic  7.07 us (5%)
    psum x1, waiting for transfers between devices, on_device(): lax.psum(pseudo.astype(jnp.bfloat16), 'rep').astype(jnp.float32)  41.8 us
    reduce_scatter x1, waiting for transfers between devices, on_device(): lax.psum_scatter(lax.dot_general(proj_grad, block_input, (((0,), (0,)), (...  40 us
    all_gather x1, waiting for transfers between devices, on_device(): gathered = lax.all_gather(weights_shard, 'fsdp', axis=0, tiled=True)  22 us
    dot_general x2, matrix products, ssd_forward(): jnp.einsum('hts,shp->thp', mixing, scaled, precision=lax.Precision.HIGHEST)  13.2 us
  transfers between devices with their start and end apart: 3, of which 3 were waited for; matrix products, arithmetic and copies ran while one was open for 5% of the time, Pallas kernels for 0%

commit v1 on v0

v1 whole, which is shorter than its diff:
```python
import functools

import jax
import jax.numpy as jnp
from jax import lax
from jax.experimental import pallas as pl
from jax.experimental.pallas import tpu as pltpu
from jax.sharding import PartitionSpec as P

STATE = 64
LOG2E = 1.4426950408889634

inner_rate = 0.002
outer_rate = 0.7
momentum_decay = 0.9

VMEM_LIMIT = 48 * 1024 * 1024
EXACT = lax.Precision.HIGHEST


def params(**more):
    return pltpu.CompilerParams(vmem_limit_bytes=VMEM_LIMIT, **more)


def whole_vmem(count):
    return [pl.BlockSpec(memory_space=pltpu.VMEM)] * count


def contract(left, right, dims, precision=None):
    return lax.dot_general(
        left, right, (dims, ((), ())), preferred_element_type=jnp.float32, precision=precision
    )


def early_kernel(cot_ref, val_ref, state_ref, cross_ref, enter_ref):
    block = cot_ref.shape[0]
    lanes = lax.broadcasted_iota(jnp.int32, (block, 2 * STATE), 1)
    rows = lax.broadcasted_iota(jnp.int32, (block, block), 0)
    cols = lax.broadcasted_iota(jnp.int32, (block, block), 1)
    causal = rows >= cols
    low = lanes < STATE
    square = (2 * STATE, 2 * STATE)
    same_head = (lax.broadcasted_iota(jnp.int32, square, 0) < STATE) == (
        lax.broadcasted_iota(jnp.int32, square, 1) < STATE
    )
    for pair in range(cot_ref.shape[1] // (2 * STATE)):
        span = slice(pair * 2 * STATE, (pair + 1) * 2 * STATE)
        cot = cot_ref[:, span]
        val = val_ref[:, span]
        zero = jnp.zeros_like(cot)
        for odd in range(2):
            one = jnp.where(low, zero, cot) if odd else jnp.where(low, cot, zero)
            cross = contract(one, val, ((1,), (1,)))
            cross_ref[2 * pair + odd] = jnp.where(causal, cross, 0.0).astype(cross_ref.dtype)
        state = state_ref[span, :]
        wide = jnp.concatenate([state, state], axis=1)
        wide = jnp.where(same_head, wide, jnp.zeros_like(wide))
        enter_ref[:, span] = contract(cot, wide, ((1,), (0,)))


def early_products(out_grad, ssd_input, state):
    block, width = out_grad.shape
    heads = width // STATE
    steps = 8
    piece = width // steps
    return pl.pallas_call(
        early_kernel,
        grid=(steps,),
        in_specs=[
            pl.BlockSpec((block, piece), lambda i: (0, i)),
            pl.BlockSpec((block, piece), lambda i: (0, i)),
            pl.BlockSpec((piece, STATE), lambda i: (i, 0)),
        ],
        out_specs=[
            pl.BlockSpec((heads // steps, block, block), lambda i: (i, 0, 0)),
            pl.BlockSpec((block, piece), lambda i: (0, i)),
        ],
        out_shape=[
            jax.ShapeDtypeStruct((heads, block, block), jnp.bfloat16),
            jax.ShapeDtypeStruct((block, width), jnp.float32),
        ],
        compiler_params=params(),
        cost_estimate=pl.CostEstimate(
            flops=2 * block * width * 4 * block, bytes_accessed=8 * block * width, transcendentals=0
        ),
        name="early_products",
    )(out_grad, ssd_input, state)


def ssd_kernel(shards, owners_ref, rows_ref, bias_ref, decay_ref, cross_ref, enter_ref, *rest):
    weight_refs = rest[:shards]
    grad_ref, grad_rel_ref, proj_ref, col_ref, out_ref = rest[shards:]
    block = rows_ref.shape[0]
    heads = bias_ref.shape[0]
    per = weight_refs[0].shape[0]
    rows_in = rows_ref[...]
    for k in range(shards):
        start = pl.multiple_of(owners_ref[k] * per, 8) if shards > 1 else 0
        proj_ref[pl.ds(start, per), :] = contract(weight_refs[k][...], rows_in, ((1,), (1,)))
    key_t = proj_ref[:STATE, :]
    query_t = proj_ref[STATE : 2 * STATE, :]
    raw = proj_ref[2 * STATE :, :] + bias_ref[...]
    step_t = jnp.maximum(raw, 0.0) + jnp.log1p(jnp.exp(-jnp.abs(raw)))
    rate = jnp.exp(decay_ref[...])
    up = lax.broadcasted_iota(jnp.int32, (block, block), 0)
    across = lax.broadcasted_iota(jnp.int32, (block, block), 1)
    before = jnp.where(up <= across, 1.0, 0.0)
    after = jnp.where(up >= across, 1.0, 0.0)
    cum_t = contract(-step_t * rate, before, ((1,), (0,)), EXACT) * LOG2E
    cum = cum_t.T
    step = step_t.T
    query = query_t.T
    key = key_t.T
    scores = contract(query, key_t, ((1,), (0,)), EXACT)
    entered = jnp.exp2(cum)
    query_twice = jnp.concatenate([query, query], axis=1)
    low = lax.broadcasted_iota(jnp.int32, (block, 2 * STATE), 1) < STATE
    head_of = lax.broadcasted_iota(jnp.int32, (block, heads), 1)
    below = lax.broadcasted_iota(jnp.int32, (block, heads), 0) < STATE

    score_grad = jnp.zeros((block, block), jnp.float32)
    query_grad = jnp.zeros((block, 2 * STATE), jnp.float32)
    row_sums = jnp.zeros((block, heads), jnp.float32)
    for h0 in range(0, heads, 4):
        left, right = [], []
        for h in range(h0, h0 + 4):
            span = cum[:, h : h + 1] - cum_t[h : h + 1, :]
            weight = cross_ref[h].astype(jnp.float32) * jnp.exp2(jnp.minimum(span, 0.0))
            score_grad = score_grad + weight * step_t[h : h + 1, :]
            mixed = weight * scores
            col_ref[h : h + 1, :] = jnp.sum(mixed, axis=0, keepdims=True)
            left.append(mixed.astype(jnp.bfloat16))
            right.append(jnp.where(head_of == h, step, 0.0).astype(jnp.bfloat16))
        for h in range(h0, h0 + 4, 2):
            gain = jnp.where(low, entered[:, h : h + 1], entered[:, h + 1 : h + 2])
            part = enter_ref[:, h * STATE : (h + 2) * STATE] * gain
            query_grad = query_grad + part
            left.append((part * query_twice).astype(jnp.bfloat16))
            right.append(
                jnp.where(head_of == jnp.where(below, h, h + 1), 1.0, 0.0).astype(jnp.bfloat16)
            )
        row_sums = row_sums + contract(
            jnp.concatenate(left, axis=1), jnp.concatenate(right, axis=0), ((1,), (0,))
        )

    cols_t = col_ref[...]
    cum_grad = row_sums.T - step_t * cols_t
    later = contract(cum_grad, after, ((1,), (0,)), EXACT)
    step_grad = cols_t - rate * later
    raw_grad = step_grad / (1.0 + jnp.exp(-raw))
    out_ref[:STATE, :] = contract(query_t, score_grad, ((1,), (0,)), EXACT)
    query_all = (query_grad[:, :STATE] + query_grad[:, STATE:]).T
    out_ref[STATE : 2 * STATE, :] = query_all + contract(key_t, score_grad, ((1,), (1,)), EXACT)
    out_ref[2 * STATE :, :] = raw_grad
    grad_ref[...] = out_ref[...].astype(jnp.bfloat16)
    if shards > 1:
        for k in range(shards):
            start = pl.multiple_of(owners_ref[k] * per, 8)
            proj_ref[k * per : (k + 1) * per, :] = out_ref[pl.ds(start, per), :]
        grad_rel_ref[...] = proj_ref[...].astype(jnp.bfloat16)
    else:
        grad_rel_ref[...] = out_ref[...].astype(jnp.bfloat16)


def ssd_backward(owners, rows_in, step_bias, decay_log, cross, enter, weights):
    block = rows_in.shape[0]
    heads = step_bias.shape[0]
    cols = sum(w.shape[0] for w in weights)
    shards = len(weights)
    return pl.pallas_call(
        functools.partial(ssd_kernel, shards),
        in_specs=[pl.BlockSpec(memory_space=pltpu.SMEM)] + whole_vmem(5 + shards),
        out_specs=whole_vmem(2),
        out_shape=[jax.ShapeDtypeStruct((cols, block), jnp.bfloat16)] * 2,
        scratch_shapes=[
            pltpu.VMEM((cols, block), jnp.float32),
            pltpu.VMEM((heads, block), jnp.float32),
            pltpu.VMEM((cols, block), jnp.float32),
        ],
        compiler_params=params(),
        cost_estimate=pl.CostEstimate(
            flops=2 * block * cols * rows_in.shape[1],
            bytes_accessed=16 * rows_in.size,
            transcendentals=heads * block * block,
        ),
        name="ssd_backward",
    )(owners, rows_in, step_bias.reshape(-1, 1), decay_log.reshape(-1, 1), cross, enter, *weights)


def slice_kernel(parts, chips, dest_ref, *refs):
    left = jnp.concatenate([r[...] for r in refs[:parts]], axis=1)
    right = jnp.concatenate([r[...] for r in refs[parts : 2 * parts]], axis=0)
    outs = refs[2 * parts : 2 * parts + chips]
    total = refs[-1]
    total[...] = contract(left, right, ((1,), (0,)))
    per = outs[0].shape[0]
    for k in range(chips):
        start = pl.multiple_of(dest_ref[k] * per, 8)
        outs[k][...] = total[pl.ds(start, per), :].astype(jnp.bfloat16)


def gradient_slices(dests, grads_t, inputs, chips):
    cols = grads_t[0].shape[0]
    width = inputs[0].shape[1]
    parts = len(inputs)
    return pl.pallas_call(
        functools.partial(slice_kernel, parts, chips),
        in_specs=[pl.BlockSpec(memory_space=pltpu.SMEM)] + whole_vmem(2 * parts),
        out_specs=whole_vmem(chips),
        out_shape=[jax.ShapeDtypeStruct((cols // chips, width), jnp.bfloat16)] * chips,
        scratch_shapes=[pltpu.VMEM((cols, width), jnp.float32)],
        compiler_params=params(),
        name="gradient_slices",
    )(dests, *grads_t, *inputs)


def line_kernel(parts, core_ref, *refs):
    total = refs[-1]
    acc = refs[0][...].astype(jnp.float32)
    for r in refs[1:parts]:
        acc = acc + r[...].astype(jnp.float32)
    total[...] = acc
    for k, out in enumerate(refs[parts:-1]):
        per = out.shape[0]
        start = pl.multiple_of(core_ref[k] * per, 8)
        out[...] = total[pl.ds(start, per), :].astype(jnp.bfloat16)


def line_sum(cores, pieces):
    rows, width = pieces[0].shape
    return pl.pallas_call(
        functools.partial(line_kernel, len(pieces)),
        in_specs=[pl.BlockSpec(memory_space=pltpu.SMEM)] + whole_vmem(len(pieces)),
        out_specs=whole_vmem(2),
        out_shape=[jax.ShapeDtypeStruct((rows // 2, width), jnp.bfloat16)] * 2,
        scratch_shapes=[pltpu.VMEM((rows, width), jnp.float32)],
        compiler_params=params(),
        name="line_sum",
    )(cores, *pieces)


def outer_kernel(parts, scale, spots_ref, mom_ref, par_ref, *refs):
    width = refs[0].shape[1]
    new_par, new_mom = refs[parts:]
    for k in range(parts):
        cols = pl.ds(pl.multiple_of(spots_ref[k] * width, 128), width)
        term = refs[k][...].astype(jnp.float32) * scale
        new_mom[:, cols] = mom_ref[:, cols] + term
        new_par[:, cols] = par_ref[:, cols] - (outer_rate * (1.0 + momentum_decay)) * term


def outer_step(spots, early_momentum, early_params, pieces, scale):
    return pl.pallas_call(
        functools.partial(outer_kernel, len(pieces), scale),
        in_specs=[pl.BlockSpec(memory_space=pltpu.SMEM)] + whole_vmem(2 + len(pieces)),
        out_specs=whole_vmem(2),
        out_shape=[jax.ShapeDtypeStruct(early_params.shape, jnp.float32)] * 2,
        compiler_params=params(),
        name="outer_step",
    )(spots, early_momentum, early_params, *pieces)


def power_of_two(n):
    return n & (n - 1) == 0


def on_device(
    replicas,
    shards,
    block_input,
    ssd_input,
    out_grad,
    start_state,
    step_bias,
    decay_log,
    local_params,
    global_params,
    momentum,
):
    local_rows = local_params[0]
    rows, depth = local_rows.shape
    own = local_rows.astype(jnp.bfloat16)
    seq_width = ssd_input.shape[1]
    chips = shards // 2
    plane = 2 * replicas
    fast = (
        shards % 2 == 0
        and shards <= 16
        and rows % 8 == 0
        and power_of_two(replicas)
        and power_of_two(chips)
        and depth % (128 * plane) == 0
    )
    rep = lax.axis_index("rep")
    spot = lax.axis_index("fsdp")
    blocks = start_state.shape[0]
    block = block_input.shape[0] // blocks

    def send(value, where):
        pairs = []
        for r in range(replicas):
            for f in range(shards):
                to_r, to_f = where(r, f)
                pairs.append((r * shards + f, to_r * shards + to_f))
        return lax.ppermute(value, ("rep", "fsdp"), pairs)

    if fast:
        ring = [2 * z for z in range(chips)] + [2 * z + 1 for z in reversed(range(chips))]
        place = [ring.index(f) for f in range(shards)]

        def around(by):
            return lambda r, f: (r, ring[(place[f] + by) % shards])

        weights = [own]
        owners = [spot]
        ring_table = jnp.array(ring, jnp.int32)
        my_place = jnp.array(place, jnp.int32)[spot]
        forward = backward = own
        for k in range(1, shards // 2 + 1):
            forward = send(forward, around(1))
            weights.append(forward)
            owners.append(ring_table[(my_place - k) % shards])
            if k < shards - k:
                backward = send(backward, around(-1))
                weights.append(backward)
                owners.append(ring_table[(my_place + k) % shards])
        owners = jnp.stack(owners).astype(jnp.int32)
    else:
        weights = [lax.all_gather(own, "fsdp", axis=0, tiled=True)]
        owners = jnp.zeros((1,), jnp.int32)

    grads_t, grads_rel_t = [], []
    for b in range(blocks):
        seq = slice(b * block, (b + 1) * block)
        cross, enter = early_products(
            out_grad[seq], ssd_input[seq], start_state[b].reshape(seq_width, STATE)
        )
        one, one_rel = ssd_backward(
            owners, block_input[seq], step_bias, decay_log, cross, enter, weights
        )
        grads_t.append(one)
        grads_rel_t.append(one_rel)
    grad_t = grads_t[0] if blocks == 1 else jnp.concatenate(grads_t, axis=1)
    grad_rel_t = grads_rel_t[0] if blocks == 1 else jnp.concatenate(grads_rel_t, axis=1)
    gathered = weights[0] if len(weights) == 1 else jnp.concatenate(weights, axis=0)
    block_grad = contract(grad_rel_t, gathered, ((0,), (0,))).astype(jnp.bfloat16)

    if not fast:
        gradient = lax.psum_scatter(
            contract(grad_t, block_input, ((1,), (0,))), "fsdp", scatter_dimension=0, tiled=True
        )
        pseudo = global_params - (local_rows - inner_rate * gradient)
        mean_pseudo = lax.psum(pseudo.astype(jnp.bfloat16), "rep").astype(jnp.float32) / replicas
        new_momentum = momentum_decay * momentum + mean_pseudo
        new_params = global_params - outer_rate * (mean_pseudo + momentum_decay * new_momentum)
        return (block_grad, new_params, new_momentum)

    shares = [own] + [
        send(own, lambda r, f, k=k: (r ^ k, f)) for k in range(1, replicas)
    ]
    shares = [s.astype(jnp.float32) for s in shares]
    while len(shares) > 1:
        shares = [shares[i] + shares[i + 1] for i in range(0, len(shares), 2)]
    early_pseudo = global_params - shares[0] / replicas
    early_momentum = momentum_decay * momentum + early_pseudo
    early_params = global_params - outer_rate * (early_pseudo + momentum_decay * early_momentum)

    core = spot % 2
    chip = spot // 2
    mine = rep * 2 + core
    width = depth // plane

    def in_plane(k):
        def where(r, f):
            q = (2 * r + f % 2) ^ k
            return q // 2, (f // 2) * 2 + q % 2

        return where

    inputs = []
    for k in range(plane):
        piece = lax.dynamic_slice_in_dim(block_input, (mine ^ k) * width, width, axis=1)
        inputs.append(send(piece, in_plane(k)) if k else piece)
    plane_grads = [grad_t] + [send(grad_t, in_plane(k)) for k in range(1, plane)]
    dests = jnp.stack([chip ^ k for k in range(chips)]).astype(jnp.int32)
    slices = gradient_slices(dests, plane_grads, inputs, chips)
    pieces = [slices[0]] + [
        send(slices[k], lambda r, f, k=k: (r, ((f // 2) ^ k) * 2 + f % 2)) for k in range(1, chips)
    ]
    cores = jnp.stack([core, 1 - core]).astype(jnp.int32)
    same, other = line_sum(cores, pieces)
    final = [same] + [
        send(other if k % 2 else same, in_plane(k)) for k in range(1, plane)
    ]
    spots = jnp.stack([mine ^ k for k in range(plane)]).astype(jnp.int32)
    new_params, new_momentum = outer_step(
        spots, early_momentum, early_params, final, inner_rate / replicas
    )
    return (block_grad, new_params, new_momentum)


def solution(mesh):
    placed = (
        P(("rep", "fsdp"), None),
        P(("rep", "fsdp"), None),
        P(("rep", "fsdp"), None),
        P(("rep", "fsdp"), None, None),
        P(),
        P(),
        P("rep", "fsdp", None),
        P("fsdp", None),
        P("fsdp", None),
    )
    return jax.shard_map(
        functools.partial(on_device, mesh.shape["rep"], mesh.shape["fsdp"]),
        mesh=mesh,
        in_specs=placed,
        out_specs=(P(("rep", "fsdp"), None), P("fsdp", None), P("fsdp", None)),
        check_vma=False,
    )
```

time: 155 us -> 102 us (0.66)
  waiting for transfers between devices: 104 us -> 24.6 us
  starting transfers between devices: 0.12 us -> 38 us
  matrix products: 22 us -> 1.43 us
  Pallas kernels: 0 us -> 16.5 us
  between operations: 13.9 us -> 5.69 us
  local copies, waits for them, and re-layouts: 7.39 us -> 12.4 us
  other arithmetic: 7.07 us -> 3.34 us
    psum x1 -> x0, waiting for transfers between devices: 41.8 us -> none  [on_device(): lax.psum(pseudo.astype(jnp.bfloat16), 'rep').astype(jnp.float32)]
    reduce_scatter x1 -> x0, waiting for transfers between devices: 40 us -> none  [on_device(): lax.psum_scatter(lax.dot_general(proj_grad, block_input, (((0,), (0,)), (...]
    ppermute x0 -> x34, starting transfers between devices: none -> 38 us  [send(): return lax.ppermute(value, ('rep', 'fsdp'), pairs)]
    ppermute x0 -> x34, waiting for transfers between devices: none -> 24.6 us  [send(): return lax.ppermute(value, ('rep', 'fsdp'), pairs)]
    all_gather x1 -> x0, waiting for transfers between devices: 22 us -> none  [on_device(): gathered = lax.all_gather(weights_shard, 'fsdp', axis=0, tiled=True)]
    dot_general x10 -> x1, matrix products: 22 us -> 1.43 us  [contract(): lax.dot_general(left, right, (dims, ((), ())), preferred_element_type=jnp...]
    pallas_call x0 -> x5, Pallas kernels: none -> 16.5 us  [the longest x1 8.64 us: ssd_backward(): pl.pallas_call(functools.partial(ssd_kernel, shards), in_specs=[pl.BlockS...]
    another operation x2 -> x3, local copies, waits for them, and re-layouts: 0.13 us -> 6.57 us  [the longest x1 4.43 us: on_device(): owners = jnp.stack(owners).astype(jnp.int32)]
  transfers between devices with their start and end apart: 3 -> 34, of which waited for: 3 -> 11; matrix products, arithmetic and copies ran while one was open for 5% -> 15% of each run, Pallas kernels for 0% -> 13%
where the time goes in v1:
time: 102 us
  starting transfers between devices  38 us (37%)
  waiting for transfers between devices  24.6 us (24%)
  Pallas kernels  16.5 us (16%)
  local copies, waits for them, and re-layouts  12.4 us (12%)
  between operations  5.69 us (6%)
  other arithmetic  3.34 us (3%)
  matrix products  1.43 us (1%)
    ppermute x34, starting transfers between devices, send(): return lax.ppermute(value, ('rep', 'fsdp'), pairs)  38 us
    ppermute x34, waiting for transfers between devices, send(): return lax.ppermute(value, ('rep', 'fsdp'), pairs)  24.6 us
    pallas_call x1, Pallas kernels, ssd_backward(): pl.pallas_call(functools.partial(ssd_kernel, shards), in_specs=[pl.BlockS...  8.64 us
    pallas_call x1, Pallas kernels, early_products(): pl.pallas_call(early_kernel, grid=(steps,), in_specs=[pl.BlockSpec((block...  4.82 us
    another operation x1, local copies, waits for them, and re-layouts, on_device(): owners = jnp.stack(owners).astype(jnp.int32)  4.43 us
    another operation x1, local copies, waits for them, and re-layouts, on_device(): start_state[b].reshape(seq_width, STATE)  2.05 us
  transfers between devices with their start and end apart: 34, of which 11 were waited for; matrix products, arithmetic and copies ran while one was open for 15% of the time, Pallas kernels for 13%

profile of v1, /device:TPU:0, one launch (start us, length us, event | category | flops | bytes accessed | tf_op | source)
XLA Modules:
  0.0 101.9 jit_solution(14994520287246744712)
XLA Ops:
  0.7 1.9 %constant_dynamic-update-slice_fusion.7 = (bf16[192,4096]{1,0:T(8,128)(2,1)}, bf16[24,4096]{1,0:T(8,128)(2,1)S(1)}) fusion(f32[1,24,4096]{2,1,0:T(8,128)} %param.17), kind=kLoop, calls=%fused_computation.12 | loop fusion | flops 98303 | bytes 786432
  2.5 3.0 %collective-permute-start = (bf16[24,4096]{1,0:T(8,128)(2,1)S(1)}, bf16[24,4096]{1,0:T(8,128)(2,1)S(1)}, u32[]{:S(2)}, u32[]{:S(2)}) collective-permute-start(bf16[24,4096]{1,0:T(8,128)(2,1)S(1)} %get-tuple-element.28.rest_0_), channel_id=1, source_target_pairs={{0,2},{1,0},{2,4},{3,1},{4,6},{5,3},{6,7},{7,5},{8,10},{9,8},{10,1... | collective-permute-start | bytes 589832 | tf_op jit(solution)/shard_map/ppermute | solution.py:305
  5.5 2.4 %collective-permute-start.9 = (bf16[24,4096]{1,0:T(8,128)(2,1)S(1)}, bf16[24,4096]{1,0:T(8,128)(2,1)}, u32[]{:S(2)}, u32[]{:S(2)}) collective-permute-start(bf16[24,4096]{1,0:T(8,128)(2,1)S(1)} %get-tuple-element.28.rest_0_), channel_id=1, source_target_pairs={{0,24},{1,25},{2,26},{3,27},{4,28},{5,29},{6,30},{7,31},{8,16},{9,... | collective-permute-start | bytes 589832 | tf_op jit(solution)/shard_map/ppermute | solution.py:305
  15.2 1.4 %copy.16.bias_ref = f32[64,1]{1,0:T(8,128)} copy(f32[64,1]{0,1:T(1,128)} %bitcast.29) | data formatting | bytes 512 | tf_op jit(solution)/shard_map/reshape | solution.py:187
  17.9 2.1 %reshape_squeeze.3.state_ref = bf16[4096,64]{1,0:T(8,128)(2,1)S(1)} reshape(bf16[1,64,4096]{2,1,0:T(8,128)(2,1)} %param.14) | data formatting | bytes 1048576 | tf_op jit(solution)/shard_map/reshape;squeeze | solution.py:336
  20.7 4.4 %stack.58.owners_ref = s32[8]{0:T(128)S(1)} concatenate(s32[1]{0:T(128)} %bitcast, s32[1]{0:T(128)} %get-tuple-element.44, s32[1]{0:T(128)} %get-tuple-element.43, s32[1]{0:T(128)} %get-tuple-element.42, s32[1]{0:T(128)} %get-tuple-element.41, s32[1]{0:T(128)} %get-tuple-element.40, s32[1]{0:T(128)} %get-tuple-element.45, s32[1]{0:T(128)} %get-tuple-element.39), dimensions={0} | concatenate | bytes 64 | tf_op jit(solution)/shard_map/stack | solution.py:327
  25.3 4.8 %early_products.1 = (bf16[64,128,128]{2,1,0:T(8,128)(2,1)S(1)}, f32[128,4096]{1,0:T(8,128)}) custom-call(bf16[128,4096]{1,0:T(8,128)(2,1)S(1)} %copy-done.1, bf16[128,4096]{1,0:T(8,128)(2,1)S(1)} %copy-done.2, bf16[4096,64]{1,0:T(8,128)(2,1)S(1)} %reshape_squeeze.3.state_ref), custom_call_target="tpu_custom_call" | custom-call | flops 536870912 | bytes 4194304 | tf_op jit(solution)/shard_map/early_products/pallas_call | solution.py:66
  30.3 1.6 %collective-permute-start.18 = (bf16[128,512]{1,0:T(8,128)(2,1)S(1)}, bf16[128,512]{1,0:T(8,128)(2,1)S(1)}, u32[]{:S(2)}, u32[]{:S(2)}) collective-permute-start(bf16[128,512]{1,0:T(8,128)(2,1)S(1)} %get-tuple-element.35), channel_id=1, source_target_pairs={{0,8},{1,9},{2,10},{3,11},{4,12},{5,13},{6,14},{7,15},{8,0},{9,1},... | collective-permute-start | bytes 393224 | tf_op jit(solution)/shard_map/ppermute | solution.py:305
  32.2 2.0 %collective-permute-start.2 = (bf16[24,4096]{1,0:T(8,128)(2,1)S(1)}, bf16[24,4096]{1,0:T(8,128)(2,1)S(1)}, u32[]{:S(2)}, u32[]{:S(2)}) collective-permute-start(bf16[24,4096]{1,0:T(8,128)(2,1)S(1)} %collective-permute-done.rest_1_), channel_id=1, source_target_pairs={{0,2},{1,0},{2,4},{3,1},{4,6},{5,3},{6,7},{7,5},{8,10},{9,8},{10,1... | collective-permute-start | bytes 589832 | tf_op jit(solution)/shard_map/ppermute | solution.py:305
  35.6 3.5 %collective-permute-done.2.rest_3_ = bf16[24,4096]{1,0:T(8,128)(2,1)S(1)} collective-permute-done((bf16[24,4096]{1,0:T(8,128)(2,1)S(1)}, bf16[24,4096]{1,0:T(8,128)(2,1)S(1)}, u32[]{:S(2)}, u32[]{:S(2)}) %collective-permute-start.2) | collective-permute-done | bytes 196640 | tf_op jit(solution)/shard_map/ppermute | solution.py:305
  39.1 2.5 %collective-permute-start.4 = (bf16[24,4096]{1,0:T(8,128)(2,1)S(1)}, bf16[24,4096]{1,0:T(8,128)(2,1)S(1)}, u32[]{:S(2)}, u32[]{:S(2)}) collective-permute-start(bf16[24,4096]{1,0:T(8,128)(2,1)S(1)} %collective-permute-done.2.rest_3_), channel_id=1, source_target_pairs={{0,2},{1,0},{2,4},{3,1},{4,6},{5,3},{6,7},{7,5},{8,10},{9,8},{10,1... | collective-permute-start | bytes 589832 | tf_op jit(solution)/shard_map/ppermute | solution.py:305
  42.5 3.2 %collective-permute-done.4.rest_5_ = bf16[24,4096]{1,0:T(8,128)(2,1)S(1)} collective-permute-done((bf16[24,4096]{1,0:T(8,128)(2,1)S(1)}, bf16[24,4096]{1,0:T(8,128)(2,1)S(1)}, u32[]{:S(2)}, u32[]{:S(2)}) %collective-permute-start.4) | collective-permute-done | bytes 196640 | tf_op jit(solution)/shard_map/ppermute | solution.py:305
  45.7 1.5 %collective-permute-start.20 = (bf16[128,512]{1,0:T(8,128)(2,1)S(1)}, bf16[128,512]{1,0:T(8,128)(2,1)S(1)}, u32[]{:S(2)}, u32[]{:S(2)}) collective-permute-start(bf16[128,512]{1,0:T(8,128)(2,1)S(1)} %get-tuple-element.33), channel_id=1, source_target_pairs={{0,16},{1,17},{2,18},{3,19},{4,20},{5,21},{6,22},{7,23},{8,24},{9,... | collective-permute-start | bytes 393224 | tf_op jit(solution)/shard_map/ppermute | solution.py:305
  47.3 2.5 %collective-permute-start.6 = (bf16[24,4096]{1,0:T(8,128)(2,1)S(1)}, bf16[24,4096]{1,0:T(8,128)(2,1)S(1)}, u32[]{:S(2)}, u32[]{:S(2)}) collective-permute-start(bf16[24,4096]{1,0:T(8,128)(2,1)S(1)} %collective-permute-done.4.rest_5_), channel_id=1, source_target_pairs={{0,2},{1,0},{2,4},{3,1},{4,6},{5,3},{6,7},{7,5},{8,10},{9,8},{10,1... | collective-permute-start | bytes 589832 | tf_op jit(solution)/shard_map/ppermute | solution.py:305
  49.7 3.2 %collective-permute-done.6.rest_7_ = bf16[24,4096]{1,0:T(8,128)(2,1)S(1)} collective-permute-done((bf16[24,4096]{1,0:T(8,128)(2,1)S(1)}, bf16[24,4096]{1,0:T(8,128)(2,1)S(1)}, u32[]{:S(2)}, u32[]{:S(2)}) %collective-permute-start.6) | collective-permute-done | bytes 196640 | tf_op jit(solution)/shard_map/ppermute | solution.py:305
  52.9 8.6 %ssd_backward.1 = (bf16[192,128]{1,0:T(8,128)(2,1)S(1)}, bf16[192,128]{1,0:T(8,128)(2,1)S(1)}) custom-call(s32[8]{0:T(128)S(1)} %stack.58.owners_ref, bf16[128,4096]{1,0:T(8,128)(2,1)S(1)} %copy-done, f32[64,1]{1,0:T(8,128)S(1)} %copy-done.3, f32[64,1]{1,0:T(8,128)S(1)} %copy-done.4, bf16[64,128,128]{2,1,0:T(8,128)(2,1)S(1)} %get-tuple-element.15.cross_ref, ...), custom_call_target="tpu_custom_call" | custom-call | flops 201326592 | bytes 8388608 | tf_op jit(solution)/shard_map/ssd_backward/pallas_call | solution.py:170
  61.6 1.8 %collective-permute-start.22 = (bf16[128,512]{1,0:T(8,128)(2,1)S(1)}, bf16[128,512]{1,0:T(8,128)(2,1)S(1)}, u32[]{:S(2)}, u32[]{:S(2)}) collective-permute-start(bf16[128,512]{1,0:T(8,128)(2,1)S(1)} %get-tuple-element.38), channel_id=1, source_target_pairs={{0,24},{1,25},{2,26},{3,27},{4,28},{5,29},{6,30},{7,31},{8,16},{9,... | collective-permute-start | bytes 393224 | tf_op jit(solution)/shard_map/ppermute | solution.py:305
  63.4 1.4 %collective-permute-start.23 = (bf16[128,512]{1,0:T(8,128)(2,1)S(1)}, bf16[128,512]{1,0:T(8,128)(2,1)S(1)}, u32[]{:S(2)}, u32[]{:S(2)}) collective-permute-start(bf16[128,512]{1,0:T(8,128)(2,1)S(1)} %get-tuple-element.31), channel_id=1, source_target_pairs={{0,25},{1,24},{2,27},{3,26},{4,29},{5,28},{6,31},{7,30},{8,17},{9,... | collective-permute-start | bytes 393224 | tf_op jit(solution)/shard_map/ppermute | solution.py:305
  64.8 1.5 %collective-permute-start.11 = (bf16[192,128]{1,0:T(8,128)(2,1)S(1)}, bf16[192,128]{1,0:T(8,128)(2,1)S(1)}, u32[]{:S(2)}, u32[]{:S(2)}) collective-permute-start(bf16[192,128]{1,0:T(8,128)(2,1)S(1)} %get-tuple-element.18.refs_0_), channel_id=1, source_target_pairs={{0,8},{1,9},{2,10},{3,11},{4,12},{5,13},{6,14},{7,15},{8,0},{9,1},... | collective-permute-start | bytes 147464 | tf_op jit(solution)/shard_map/ppermute | solution.py:305
  66.8 2.2 %collective-permute-done.22.refs_14_ = bf16[128,512]{1,0:T(8,128)(2,1)S(1)} collective-permute-done((bf16[128,512]{1,0:T(8,128)(2,1)S(1)}, bf16[128,512]{1,0:T(8,128)(2,1)S(1)}, u32[]{:S(2)}, u32[]{:S(2)}) %collective-permute-start.22) | collective-permute-done | bytes 131104 | tf_op jit(solution)/shard_map/ppermute | solution.py:305
  69.4 2.2 %collective-permute-done.23.refs_15_ = bf16[128,512]{1,0:T(8,128)(2,1)S(1)} collective-permute-done((bf16[128,512]{1,0:T(8,128)(2,1)S(1)}, bf16[128,512]{1,0:T(8,128)(2,1)S(1)}, u32[]{:S(2)}, u32[]{:S(2)}) %collective-permute-start.23) | collective-permute-done | bytes 131104 | tf_op jit(solution)/shard_map/ppermute | solution.py:305
  71.9 2.3 %collective-permute-start.15 = (bf16[192,128]{1,0:T(8,128)(2,1)S(1)}, bf16[192,128]{1,0:T(8,128)(2,1)S(1)}, u32[]{:S(2)}, u32[]{:S(2)}) collective-permute-start(bf16[192,128]{1,0:T(8,128)(2,1)S(1)} %get-tuple-element.18.refs_0_), channel_id=1, source_target_pairs={{0,24},{1,25},{2,26},{3,27},{4,28},{5,29},{6,30},{7,31},{8,16},{9,... | collective-permute-start | bytes 147464 | tf_op jit(solution)/shard_map/ppermute | solution.py:305
  75.3 2.1 %collective-permute-done.15.refs_6_ = bf16[192,128]{1,0:T(8,128)(2,1)S(1)} collective-permute-done((bf16[192,128]{1,0:T(8,128)(2,1)S(1)}, bf16[192,128]{1,0:T(8,128)(2,1)S(1)}, u32[]{:S(2)}, u32[]{:S(2)}) %collective-permute-start.15) | collective-permute-done | bytes 49184 | tf_op jit(solution)/shard_map/ppermute | solution.py:305
  77.4 1.4 %collective-permute-done.16.refs_7_ = bf16[192,128]{1,0:T(8,128)(2,1)S(1)} collective-permute-done((bf16[192,128]{1,0:T(8,128)(2,1)S(1)}, bf16[192,128]{1,0:T(8,128)(2,1)S(1)}, u32[]{:S(2)}, u32[]{:S(2)}) %collective-permute-start.16) | collective-permute-done | bytes 49184 | tf_op jit(solution)/shard_map/ppermute | solution.py:305
  79.8 2.6 %collective-permute-start.24 = (bf16[48,512]{1,0:T(8,128)(2,1)S(1)}, bf16[48,512]{1,0:T(8,128)(2,1)S(1)}, u32[]{:S(2)}, u32[]{:S(2)}) collective-permute-start(bf16[48,512]{1,0:T(8,128)(2,1)S(1)} %get-tuple-element.20), channel_id=1, source_target_pairs={{0,2},{1,3},{2,0},{3,1},{4,6},{5,7},{6,4},{7,5},{8,10},{9,11},{10,... | collective-permute-start | bytes 147464 | tf_op jit(solution)/shard_map/ppermute | solution.py:305
  82.4 2.8 %collective-permute-start.25 = (bf16[48,512]{1,0:T(8,128)(2,1)S(1)}, bf16[48,512]{1,0:T(8,128)(2,1)S(1)}, u32[]{:S(2)}, u32[]{:S(2)}) collective-permute-start(bf16[48,512]{1,0:T(8,128)(2,1)S(1)} %get-tuple-element.21), channel_id=1, source_target_pairs={{0,4},{1,5},{2,6},{3,7},{4,0},{5,1},{6,2},{7,3},{8,12},{9,13},{10,... | collective-permute-start | bytes 147464 | tf_op jit(solution)/shard_map/ppermute | solution.py:305
  85.3 3.0 %collective-permute-done.25.refs_2_ = bf16[48,512]{1,0:T(8,128)(2,1)S(1)} collective-permute-done((bf16[48,512]{1,0:T(8,128)(2,1)S(1)}, bf16[48,512]{1,0:T(8,128)(2,1)S(1)}, u32[]{:S(2)}, u32[]{:S(2)}) %collective-permute-start.25) | collective-permute-done | bytes 49184 | tf_op jit(solution)/shard_map/ppermute | solution.py:305
  88.3 2.8 %collective-permute-done.26.refs_3_ = bf16[48,512]{1,0:T(8,128)(2,1)S(1)} collective-permute-done((bf16[48,512]{1,0:T(8,128)(2,1)S(1)}, bf16[48,512]{1,0:T(8,128)(2,1)S(1)}, u32[]{:S(2)}, u32[]{:S(2)}) %collective-permute-start.26) | collective-permute-done | bytes 49184 | tf_op jit(solution)/shard_map/ppermute | solution.py:305
  93.9 1.5 %collective-permute-start.31 = (bf16[24,512]{1,0:T(8,128)(2,1)S(1)}, bf16[24,512]{1,0:T(8,128)(2,1)S(1)}, u32[]{:S(2)}, u32[]{:S(2)}) collective-permute-start(bf16[24,512]{1,0:T(8,128)(2,1)S(1)} %get-tuple-element.24), channel_id=1, source_target_pairs={{0,17},{1,16},{2,19},{3,18},{4,21},{5,20},{6,23},{7,22},{8,25},{9,... | collective-permute-start | bytes 73736 | tf_op jit(solution)/shard_map/ppermute | solution.py:305
  96.0 2.1 %collective-permute-start.33 = (bf16[24,512]{1,0:T(8,128)(2,1)S(1)}, bf16[24,512]{1,0:T(8,128)(2,1)S(1)}, u32[]{:S(2)}, u32[]{:S(2)}) collective-permute-start(bf16[24,512]{1,0:T(8,128)(2,1)S(1)} %get-tuple-element.24), channel_id=1, source_target_pairs={{0,25},{1,24},{2,27},{3,26},{4,29},{5,28},{6,31},{7,30},{8,17},{9,... | collective-permute-start | bytes 73736 | tf_op jit(solution)/shard_map/ppermute | solution.py:305
  98.1 1.4 %convolution_convert_fusion = bf16[128,4096]{1,0:T(8,128)(2,1)} fusion(bf16[192,128]{1,0:T(8,128)(2,1)S(1)} %get-tuple-element.17, bf16[192,4096]{1,0:T(8,128)(2,1)S(1)} %constant_dynamic-update-slice_fusion), kind=kOutput, calls=%fused_computation | convolution fusion | flops 201850880 | bytes 2670592 | tf_op jit(solution)/shard_map/dot_general | solution.py:30
  100.4 1.5 %outer_step.1 = (f32[24,4096]{1,0:T(8,128)}, f32[24,4096]{1,0:T(8,128)}) custom-call(s32[8]{0:T(128)S(1)} %stack.67.spots_ref, f32[24,4096]{1,0:T(8,128)S(1)} %get-tuple-element.30.mom_ref, f32[24,4096]{1,0:T(8,128)S(1)} %get-tuple-element.29.par_ref, bf16[24,512]{1,0:T(8,128)(2,1)S(1)} %get-tuple-element.23.refs_0_, ...), custom_call_target="tpu_custom_call" | custom-call | tf_op jit(solution)/shard_map/outer_step/pallas_call | solution.py:253
  (79 shorter events, 14.9 us)
Async XLA Ops:
  2.5 27.7 %collective-permute-start = (bf16[24,4096]{1,0:T(8,128)(2,1)S(1)}, bf16[24,4096]{1,0:T(8,128)(2,1)S(1)}, u32[]{:S(2)}, u32[]{:S(2)}) collective-permute-start(bf16[24,4096]{1,0:T(8,128)(2,1)S(1)} %get-tuple-element.28.rest_0_), channel_id=1, source_target_pairs={{0,2},{1,0},{2,4},{3,1},{4,6},{5,3},{6,7},{7,5},{8,10},{9,8},{10,1... | collective-permute-start | bytes 589832 | tf_op jit(solution)/shard_map/ppermute | solution.py:305
  5.5 24.8 %collective-permute-start.1 = (bf16[24,4096]{1,0:T(8,128)(2,1)S(1)}, bf16[24,4096]{1,0:T(8,128)(2,1)}, u32[]{:S(2)}, u32[]{:S(2)}) collective-permute-start(bf16[24,4096]{1,0:T(8,128)(2,1)S(1)} %get-tuple-element.28.rest_0_), channel_id=1, source_target_pairs={{0,1},{1,3},{2,0},{3,5},{4,2},{5,7},{6,4},{7,6},{8,9},{9,11},{10,8... | collective-permute-start | bytes 589832 | tf_op jit(solution)/shard_map/ppermute | solution.py:305
  5.5 26.3 %collective-permute-start.9 = (bf16[24,4096]{1,0:T(8,128)(2,1)S(1)}, bf16[24,4096]{1,0:T(8,128)(2,1)}, u32[]{:S(2)}, u32[]{:S(2)}) collective-permute-start(bf16[24,4096]{1,0:T(8,128)(2,1)S(1)} %get-tuple-element.28.rest_0_), channel_id=1, source_target_pairs={{0,24},{1,25},{2,26},{3,27},{4,28},{5,29},{6,30},{7,31},{8,16},{9,... | collective-permute-start | bytes 589832 | tf_op jit(solution)/shard_map/ppermute | solution.py:305
  8.0 24.2 %collective-permute-start.8 = (bf16[24,4096]{1,0:T(8,128)(2,1)S(1)}, bf16[24,4096]{1,0:T(8,128)(2,1)}, u32[]{:S(2)}, u32[]{:S(2)}) collective-permute-start(bf16[24,4096]{1,0:T(8,128)(2,1)S(1)} %get-tuple-element.28.rest_0_), channel_id=1, source_target_pairs={{0,16},{1,17},{2,18},{3,19},{4,20},{5,21},{6,22},{7,23},{8,24},{9,... | collective-permute-start | bytes 589832 | tf_op jit(solution)/shard_map/ppermute | solution.py:305
  8.5 25.7 %collective-permute-start.7 = (bf16[24,4096]{1,0:T(8,128)(2,1)S(1)}, bf16[24,4096]{1,0:T(8,128)(2,1)}, u32[]{:S(2)}, u32[]{:S(2)}) collective-permute-start(bf16[24,4096]{1,0:T(8,128)(2,1)S(1)} %get-tuple-element.28.rest_0_), channel_id=1, source_target_pairs={{0,8},{1,9},{2,10},{3,11},{4,12},{5,13},{6,14},{7,15},{8,0},{9,1},... | collective-permute-start | bytes 589832 | tf_op jit(solution)/shard_map/ppermute | solution.py:305
  30.2 31.4 %collective-permute-start.17 = (bf16[128,512]{1,0:T(8,128)(2,1)S(1)}, bf16[128,512]{1,0:T(8,128)(2,1)S(1)}, u32[]{:S(2)}, u32[]{:S(2)}) collective-permute-start(bf16[128,512]{1,0:T(8,128)(2,1)S(1)} %get-tuple-element.36), channel_id=1, source_target_pairs={{0,1},{1,0},{2,3},{3,2},{4,5},{5,4},{6,7},{7,6},{8,9},{9,8},{10,11... | collective-permute-start | bytes 393224 | tf_op jit(solution)/shard_map/ppermute | solution.py:305
  30.3 33.0 %collective-permute-start.18 = (bf16[128,512]{1,0:T(8,128)(2,1)S(1)}, bf16[128,512]{1,0:T(8,128)(2,1)S(1)}, u32[]{:S(2)}, u32[]{:S(2)}) collective-permute-start(bf16[128,512]{1,0:T(8,128)(2,1)S(1)} %get-tuple-element.35), channel_id=1, source_target_pairs={{0,8},{1,9},{2,10},{3,11},{4,12},{5,13},{6,14},{7,15},{8,0},{9,1},... | collective-permute-start | bytes 393224 | tf_op jit(solution)/shard_map/ppermute | solution.py:305
  31.9 32.9 %collective-permute-start.19 = (bf16[128,512]{1,0:T(8,128)(2,1)S(1)}, bf16[128,512]{1,0:T(8,128)(2,1)S(1)}, u32[]{:S(2)}, u32[]{:S(2)}) collective-permute-start(bf16[128,512]{1,0:T(8,128)(2,1)S(1)} %get-tuple-element.34), channel_id=1, source_target_pairs={{0,9},{1,8},{2,11},{3,10},{4,13},{5,12},{6,15},{7,14},{8,1},{9,0},... | collective-permute-start | bytes 393224 | tf_op jit(solution)/shard_map/ppermute | solution.py:305
  32.2 6.9 %collective-permute-start.2 = (bf16[24,4096]{1,0:T(8,128)(2,1)S(1)}, bf16[24,4096]{1,0:T(8,128)(2,1)S(1)}, u32[]{:S(2)}, u32[]{:S(2)}) collective-permute-start(bf16[24,4096]{1,0:T(8,128)(2,1)S(1)} %collective-permute-done.rest_1_), channel_id=1, source_target_pairs={{0,2},{1,0},{2,4},{3,1},{4,6},{5,3},{6,7},{7,5},{8,10},{9,8},{10,1... | collective-permute-start | bytes 589832 | tf_op jit(solution)/shard_map/ppermute | solution.py:305
  34.2 7.4 %collective-permute-start.3 = (bf16[24,4096]{1,0:T(8,128)(2,1)}, bf16[24,4096]{1,0:T(8,128)(2,1)S(1)}, u32[]{:S(2)}, u32[]{:S(2)}) collective-permute-start(bf16[24,4096]{1,0:T(8,128)(2,1)} %collective-permute-done.1.rest_2_), channel_id=1, source_target_pairs={{0,1},{1,3},{2,0},{3,5},{4,2},{5,7},{6,4},{7,6},{8,9},{9,11},{10,8... | collective-permute-start | bytes 589832 | tf_op jit(solution)/shard_map/ppermute | solution.py:305
  39.1 6.6 %collective-permute-start.4 = (bf16[24,4096]{1,0:T(8,128)(2,1)S(1)}, bf16[24,4096]{1,0:T(8,128)(2,1)S(1)}, u32[]{:S(2)}, u32[]{:S(2)}) collective-permute-start(bf16[24,4096]{1,0:T(8,128)(2,1)S(1)} %collective-permute-done.2.rest_3_), channel_id=1, source_target_pairs={{0,2},{1,0},{2,4},{3,1},{4,6},{5,3},{6,7},{7,5},{8,10},{9,8},{10,1... | collective-permute-start | bytes 589832 | tf_op jit(solution)/shard_map/ppermute | solution.py:305
  41.6 5.7 %collective-permute-start.5 = (bf16[24,4096]{1,0:T(8,128)(2,1)S(1)}, bf16[24,4096]{1,0:T(8,128)(2,1)S(1)}, u32[]{:S(2)}, u32[]{:S(2)}) collective-permute-start(bf16[24,4096]{1,0:T(8,128)(2,1)S(1)} %collective-permute-done.3.rest_4_), channel_id=1, source_target_pairs={{0,1},{1,3},{2,0},{3,5},{4,2},{5,7},{6,4},{7,6},{8,9},{9,11},{10,8... | collective-permute-start | bytes 589832 | tf_op jit(solution)/shard_map/ppermute | solution.py:305
  45.7 19.1 %collective-permute-start.20 = (bf16[128,512]{1,0:T(8,128)(2,1)S(1)}, bf16[128,512]{1,0:T(8,128)(2,1)S(1)}, u32[]{:S(2)}, u32[]{:S(2)}) collective-permute-start(bf16[128,512]{1,0:T(8,128)(2,1)S(1)} %get-tuple-element.33), channel_id=1, source_target_pairs={{0,16},{1,17},{2,18},{3,19},{4,20},{5,21},{6,22},{7,23},{8,24},{9,... | collective-permute-start | bytes 393224 | tf_op jit(solution)/shard_map/ppermute | solution.py:305
  47.3 5.6 %collective-permute-start.6 = (bf16[24,4096]{1,0:T(8,128)(2,1)S(1)}, bf16[24,4096]{1,0:T(8,128)(2,1)S(1)}, u32[]{:S(2)}, u32[]{:S(2)}) collective-permute-start(bf16[24,4096]{1,0:T(8,128)(2,1)S(1)} %collective-permute-done.4.rest_5_), channel_id=1, source_target_pairs={{0,2},{1,0},{2,4},{3,1},{4,6},{5,3},{6,7},{7,5},{8,10},{9,8},{10,1... | collective-permute-start | bytes 589832 | tf_op jit(solution)/shard_map/ppermute | solution.py:305
  52.9 13.5 %collective-permute-start.21 = (bf16[128,512]{1,0:T(8,128)(2,1)S(1)}, bf16[128,512]{1,0:T(8,128)(2,1)S(1)}, u32[]{:S(2)}, u32[]{:S(2)}) collective-permute-start(bf16[128,512]{1,0:T(8,128)(2,1)S(1)} %get-tuple-element.32), channel_id=1, source_target_pairs={{0,17},{1,16},{2,19},{3,18},{4,21},{5,20},{6,23},{7,22},{8,25},{9,... | collective-permute-start | bytes 393224 | tf_op jit(solution)/shard_map/ppermute | solution.py:305
  61.6 7.3 %collective-permute-start.22 = (bf16[128,512]{1,0:T(8,128)(2,1)S(1)}, bf16[128,512]{1,0:T(8,128)(2,1)S(1)}, u32[]{:S(2)}, u32[]{:S(2)}) collective-permute-start(bf16[128,512]{1,0:T(8,128)(2,1)S(1)} %get-tuple-element.38), channel_id=1, source_target_pairs={{0,24},{1,25},{2,26},{3,27},{4,28},{5,29},{6,30},{7,31},{8,16},{9,... | collective-permute-start | bytes 393224 | tf_op jit(solution)/shard_map/ppermute | solution.py:305
  63.4 8.2 %collective-permute-start.23 = (bf16[128,512]{1,0:T(8,128)(2,1)S(1)}, bf16[128,512]{1,0:T(8,128)(2,1)S(1)}, u32[]{:S(2)}, u32[]{:S(2)}) collective-permute-start(bf16[128,512]{1,0:T(8,128)(2,1)S(1)} %get-tuple-element.31), channel_id=1, source_target_pairs={{0,25},{1,24},{2,27},{3,26},{4,29},{5,28},{6,31},{7,30},{8,17},{9,... | collective-permute-start | bytes 393224 | tf_op jit(solution)/shard_map/ppermute | solution.py:305
  64.8 7.1 %collective-permute-start.10 = (bf16[192,128]{1,0:T(8,128)(2,1)S(1)}, bf16[192,128]{1,0:T(8,128)(2,1)S(1)}, u32[]{:S(2)}, u32[]{:S(2)}) collective-permute-start(bf16[192,128]{1,0:T(8,128)(2,1)S(1)} %get-tuple-element.18.refs_0_), channel_id=1, source_target_pairs={{0,1},{1,0},{2,3},{3,2},{4,5},{5,4},{6,7},{7,6},{8,9},{9,8},{10,11... | collective-permute-start | bytes 147464 | tf_op jit(solution)/shard_map/ppermute | solution.py:305
  64.8 9.4 %collective-permute-start.11 = (bf16[192,128]{1,0:T(8,128)(2,1)S(1)}, bf16[192,128]{1,0:T(8,128)(2,1)S(1)}, u32[]{:S(2)}, u32[]{:S(2)}) collective-permute-start(bf16[192,128]{1,0:T(8,128)(2,1)S(1)} %get-tuple-element.18.refs_0_), channel_id=1, source_target_pairs={{0,8},{1,9},{2,10},{3,11},{4,12},{5,13},{6,14},{7,15},{8,0},{9,1},... | collective-permute-start | bytes 147464 | tf_op jit(solution)/shard_map/ppermute | solution.py:305
  66.4 8.8 %collective-permute-start.12 = (bf16[192,128]{1,0:T(8,128)(2,1)S(1)}, bf16[192,128]{1,0:T(8,128)(2,1)S(1)}, u32[]{:S(2)}, u32[]{:S(2)}) collective-permute-start(bf16[192,128]{1,0:T(8,128)(2,1)S(1)} %get-tuple-element.18.refs_0_), channel_id=1, source_target_pairs={{0,9},{1,8},{2,11},{3,10},{4,13},{5,12},{6,15},{7,14},{8,1},{9,0},... | collective-permute-start | bytes 147464 | tf_op jit(solution)/shard_map/ppermute | solution.py:305
  68.9 6.3 %collective-permute-start.13 = (bf16[192,128]{1,0:T(8,128)(2,1)S(1)}, bf16[192,128]{1,0:T(8,128)(2,1)S(1)}, u32[]{:S(2)}, u32[]{:S(2)}) collective-permute-start(bf16[192,128]{1,0:T(8,128)(2,1)S(1)} %get-tuple-element.18.refs_0_), channel_id=1, source_target_pairs={{0,16},{1,17},{2,18},{3,19},{4,20},{5,21},{6,22},{7,23},{8,24},{9,... | collective-permute-start | bytes 147464 | tf_op jit(solution)/shard_map/ppermute | solution.py:305
  71.9 5.5 %collective-permute-start.15 = (bf16[192,128]{1,0:T(8,128)(2,1)S(1)}, bf16[192,128]{1,0:T(8,128)(2,1)S(1)}, u32[]{:S(2)}, u32[]{:S(2)}) collective-permute-start(bf16[192,128]{1,0:T(8,128)(2,1)S(1)} %get-tuple-element.18.refs_0_), channel_id=1, source_target_pairs={{0,24},{1,25},{2,26},{3,27},{4,28},{5,29},{6,30},{7,31},{8,16},{9,... | collective-permute-start | bytes 147464 | tf_op jit(solution)/shard_map/ppermute | solution.py:305
  74.2 4.6 %collective-permute-start.16 = (bf16[192,128]{1,0:T(8,128)(2,1)S(1)}, bf16[192,128]{1,0:T(8,128)(2,1)S(1)}, u32[]{:S(2)}, u32[]{:S(2)}) collective-permute-start(bf16[192,128]{1,0:T(8,128)(2,1)S(1)} %get-tuple-element.18.refs_0_), channel_id=1, source_target_pairs={{0,25},{1,24},{2,27},{3,26},{4,29},{5,28},{6,31},{7,30},{8,17},{9,... | collective-permute-start | bytes 147464 | tf_op jit(solution)/shard_map/ppermute | solution.py:305
  79.8 5.5 %collective-permute-start.24 = (bf16[48,512]{1,0:T(8,128)(2,1)S(1)}, bf16[48,512]{1,0:T(8,128)(2,1)S(1)}, u32[]{:S(2)}, u32[]{:S(2)}) collective-permute-start(bf16[48,512]{1,0:T(8,128)(2,1)S(1)} %get-tuple-element.20), channel_id=1, source_target_pairs={{0,2},{1,3},{2,0},{3,1},{4,6},{5,7},{6,4},{7,5},{8,10},{9,11},{10,... | collective-permute-start | bytes 147464 | tf_op jit(solution)/shard_map/ppermute | solution.py:305
  82.4 5.9 %collective-permute-start.25 = (bf16[48,512]{1,0:T(8,128)(2,1)S(1)}, bf16[48,512]{1,0:T(8,128)(2,1)S(1)}, u32[]{:S(2)}, u32[]{:S(2)}) collective-permute-start(bf16[48,512]{1,0:T(8,128)(2,1)S(1)} %get-tuple-element.21), channel_id=1, source_target_pairs={{0,4},{1,5},{2,6},{3,7},{4,0},{5,1},{6,2},{7,3},{8,12},{9,13},{10,... | collective-permute-start | bytes 147464 | tf_op jit(solution)/shard_map/ppermute | solution.py:305
  85.2 5.9 %collective-permute-start.26 = (bf16[48,512]{1,0:T(8,128)(2,1)S(1)}, bf16[48,512]{1,0:T(8,128)(2,1)S(1)}, u32[]{:S(2)}, u32[]{:S(2)}) collective-permute-start(bf16[48,512]{1,0:T(8,128)(2,1)S(1)} %get-tuple-element.22), channel_id=1, source_target_pairs={{0,6},{1,7},{2,4},{3,5},{4,2},{5,3},{6,0},{7,1},{8,14},{9,15},{10,... | collective-permute-start | bytes 147464 | tf_op jit(solution)/shard_map/ppermute | solution.py:305
  91.8 4.2 %collective-permute-start.28 = (bf16[24,512]{1,0:T(8,128)(2,1)S(1)}, bf16[24,512]{1,0:T(8,128)(2,1)S(1)}, u32[]{:S(2)}, u32[]{:S(2)}) collective-permute-start(bf16[24,512]{1,0:T(8,128)(2,1)S(1)} %get-tuple-element.23.refs_0_), channel_id=1, source_target_pairs={{0,8},{1,9},{2,10},{3,11},{4,12},{5,13},{6,14},{7,15},{8,0},{9,1},... | collective-permute-start | bytes 73736 | tf_op jit(solution)/shard_map/ppermute | solution.py:305
  92.4 7.2 %collective-permute-start.29 = (bf16[24,512]{1,0:T(8,128)(2,1)S(1)}, bf16[24,512]{1,0:T(8,128)(2,1)S(1)}, u32[]{:S(2)}, u32[]{:S(2)}) collective-permute-start(bf16[24,512]{1,0:T(8,128)(2,1)S(1)} %get-tuple-element.24), channel_id=1, source_target_pairs={{0,9},{1,8},{2,11},{3,10},{4,13},{5,12},{6,15},{7,14},{8,1},{9,0},... | collective-permute-start | bytes 73736 | tf_op jit(solution)/shard_map/ppermute | solution.py:305
  93.7 5.9 %collective-permute-start.30 = (bf16[24,512]{1,0:T(8,128)(2,1)S(1)}, bf16[24,512]{1,0:T(8,128)(2,1)S(1)}, u32[]{:S(2)}, u32[]{:S(2)}) collective-permute-start(bf16[24,512]{1,0:T(8,128)(2,1)S(1)} %get-tuple-element.23.refs_0_), channel_id=1, source_target_pairs={{0,16},{1,17},{2,18},{3,19},{4,20},{5,21},{6,22},{7,23},{8,24},{9,... | collective-permute-start | bytes 73736 | tf_op jit(solution)/shard_map/ppermute | solution.py:305
  93.9 5.7 %collective-permute-start.31 = (bf16[24,512]{1,0:T(8,128)(2,1)S(1)}, bf16[24,512]{1,0:T(8,128)(2,1)S(1)}, u32[]{:S(2)}, u32[]{:S(2)}) collective-permute-start(bf16[24,512]{1,0:T(8,128)(2,1)S(1)} %get-tuple-element.24), channel_id=1, source_target_pairs={{0,17},{1,16},{2,19},{3,18},{4,21},{5,20},{6,23},{7,22},{8,25},{9,... | collective-permute-start | bytes 73736 | tf_op jit(solution)/shard_map/ppermute | solution.py:305
  95.4 5.0 %collective-permute-start.32 = (bf16[24,512]{1,0:T(8,128)(2,1)S(1)}, bf16[24,512]{1,0:T(8,128)(2,1)S(1)}, u32[]{:S(2)}, u32[]{:S(2)}) collective-permute-start(bf16[24,512]{1,0:T(8,128)(2,1)S(1)} %get-tuple-element.23.refs_0_), channel_id=1, source_target_pairs={{0,24},{1,25},{2,26},{3,27},{4,28},{5,29},{6,30},{7,31},{8,16},{9,... | collective-permute-start | bytes 73736 | tf_op jit(solution)/shard_map/ppermute | solution.py:305
  96.0 4.4 %collective-permute-start.33 = (bf16[24,512]{1,0:T(8,128)(2,1)S(1)}, bf16[24,512]{1,0:T(8,128)(2,1)S(1)}, u32[]{:S(2)}, u32[]{:S(2)}) collective-permute-start(bf16[24,512]{1,0:T(8,128)(2,1)S(1)} %get-tuple-element.24), channel_id=1, source_target_pairs={{0,25},{1,24},{2,27},{3,26},{4,29},{5,28},{6,31},{7,30},{8,17},{9,... | collective-permute-start | bytes 73736 | tf_op jit(solution)/shard_map/ppermute | solution.py:305
  (11 other events, 136.7 us)

commit v2 on v1

v2 whole, which is shorter than its diff:
```python
import functools

import jax
import jax.numpy as jnp
from jax import lax
from jax.experimental import pallas as pl
from jax.experimental.pallas import tpu as pltpu
from jax.sharding import PartitionSpec as P

STATE = 64
LOG2E = 1.4426950408889634

inner_rate = 0.002
outer_rate = 0.7
momentum_decay = 0.9

VMEM_LIMIT = 48 * 1024 * 1024
EXACT = lax.Precision.HIGHEST


def params(**more):
    return pltpu.CompilerParams(vmem_limit_bytes=VMEM_LIMIT, **more)


def whole_vmem(count):
    return [pl.BlockSpec(memory_space=pltpu.VMEM)] * count


def contract(left, right, dims, precision=None):
    return lax.dot_general(
        left, right, (dims, ((), ())), preferred_element_type=jnp.float32, precision=precision
    )


def early_kernel(cot_ref, val_ref, state_ref, cross_ref, enter_ref):
    block = cot_ref.shape[0]
    lanes = lax.broadcasted_iota(jnp.int32, (block, 2 * STATE), 1)
    rows = lax.broadcasted_iota(jnp.int32, (block, block), 0)
    cols = lax.broadcasted_iota(jnp.int32, (block, block), 1)
    causal = rows >= cols
    low = lanes < STATE
    square = (2 * STATE, 2 * STATE)
    same_head = (lax.broadcasted_iota(jnp.int32, square, 0) < STATE) == (
        lax.broadcasted_iota(jnp.int32, square, 1) < STATE
    )
    for pair in range(cot_ref.shape[1] // (2 * STATE)):
        span = slice(pair * 2 * STATE, (pair + 1) * 2 * STATE)
        cot = cot_ref[:, span]
        val = val_ref[:, span]
        zero = jnp.zeros_like(cot)
        for odd in range(2):
            one = jnp.where(low, zero, cot) if odd else jnp.where(low, cot, zero)
            cross = contract(one, val, ((1,), (1,)))
            cross_ref[2 * pair + odd] = jnp.where(causal, cross, 0.0).astype(cross_ref.dtype)
        state = state_ref[span, :]
        wide = jnp.concatenate([state, state], axis=1)
        wide = jnp.where(same_head, wide, jnp.zeros_like(wide))
        enter_ref[:, span] = contract(cot, wide, ((1,), (0,)))


def early_products(out_grad, ssd_input, state):
    block, width = out_grad.shape
    heads = width // STATE
    steps = 8
    piece = width // steps
    return pl.pallas_call(
        early_kernel,
        grid=(steps,),
        in_specs=[
            pl.BlockSpec((block, piece), lambda i: (0, i)),
            pl.BlockSpec((block, piece), lambda i: (0, i)),
            pl.BlockSpec((piece, STATE), lambda i: (i, 0)),
        ],
        out_specs=[
            pl.BlockSpec((heads // steps, block, block), lambda i: (i, 0, 0)),
            pl.BlockSpec((block, piece), lambda i: (0, i)),
        ],
        out_shape=[
            jax.ShapeDtypeStruct((heads, block, block), jnp.bfloat16),
            jax.ShapeDtypeStruct((block, width), jnp.float32),
        ],
        compiler_params=params(),
        cost_estimate=pl.CostEstimate(
            flops=2 * block * width * 4 * block, bytes_accessed=8 * block * width, transcendentals=0
        ),
        name="early_products",
    )(out_grad, ssd_input, state)


def stacked(refs):
    if len(refs) == 1:
        return refs[0][...]
    return jnp.concatenate([r[...].astype(jnp.float32) for r in refs], axis=0).astype(jnp.bfloat16)


def shard_rows(where_ref, k, rows):
    return pl.ds(pl.multiple_of((where_ref[1] ^ k) * rows, 8), rows)


def ssd_kernel(order, replicas, where_ref, rows_ref, bias_ref, decay_ref, cross_ref, enter_ref, *rest):
    shards = len(order)
    weight_refs = rest[:shards]
    grad_ref, send_ref, proj_ref, col_ref, out_ref = rest[shards:]
    block = rows_ref.shape[0]
    heads = bias_ref.shape[1]
    per = weight_refs[0].shape[0]
    arrived = contract(stacked(weight_refs), rows_ref[...], ((1,), (1,)))
    for at, k in enumerate(order):
        if shards > 1:
            proj_ref[shard_rows(where_ref, k, per), :] = arrived[at * per : (at + 1) * per]
        else:
            proj_ref[...] = arrived
    key_t = proj_ref[:STATE, :]
    query_t = proj_ref[STATE : 2 * STATE, :]
    bias_t = jnp.broadcast_to(bias_ref[...], (block, heads)).T
    rate = jnp.exp(jnp.broadcast_to(decay_ref[...], (block, heads)).T)
    raw = proj_ref[2 * STATE :, :] + bias_t
    step_t = jnp.maximum(raw, 0.0) + jnp.log1p(jnp.exp(-jnp.abs(raw)))
    up = lax.broadcasted_iota(jnp.int32, (block, block), 0)
    across = lax.broadcasted_iota(jnp.int32, (block, block), 1)
    before = jnp.where(up <= across, 1.0, 0.0)
    after = jnp.where(up >= across, 1.0, 0.0)
    cum_t = contract(-step_t * rate, before, ((1,), (0,)), EXACT) * LOG2E
    cum = cum_t.T
    step = step_t.T
    query = query_t.T
    scores = contract(query, key_t, ((1,), (0,)), EXACT)
    entered = jnp.exp2(cum)
    query_twice = jnp.concatenate([query, query], axis=1)
    low = lax.broadcasted_iota(jnp.int32, (block, 2 * STATE), 1) < STATE
    head_of = lax.broadcasted_iota(jnp.int32, (block, heads), 1)
    below = lax.broadcasted_iota(jnp.int32, (block, heads), 0) < STATE

    score_grad = jnp.zeros((block, block), jnp.float32)
    query_grad = jnp.zeros((block, 2 * STATE), jnp.float32)
    row_sums = jnp.zeros((block, heads), jnp.float32)
    for h0 in range(0, heads, 4):
        left, right = [], []
        for h in range(h0, h0 + 4):
            span = cum[:, h : h + 1] - cum_t[h : h + 1, :]
            weight = cross_ref[h].astype(jnp.float32) * jnp.exp2(jnp.minimum(span, 0.0))
            score_grad = score_grad + weight * step_t[h : h + 1, :]
            mixed = weight * scores
            col_ref[h : h + 1, :] = jnp.sum(mixed, axis=0, keepdims=True)
            left.append(mixed.astype(jnp.bfloat16))
            right.append(jnp.where(head_of == h, step, 0.0).astype(jnp.bfloat16))
        for h in range(h0, h0 + 4, 2):
            gain = jnp.where(low, entered[:, h : h + 1], entered[:, h + 1 : h + 2])
            part = enter_ref[:, h * STATE : (h + 2) * STATE] * gain
            query_grad = query_grad + part
            left.append((part * query_twice).astype(jnp.bfloat16))
            right.append(
                jnp.where(head_of == jnp.where(below, h, h + 1), 1.0, 0.0).astype(jnp.bfloat16)
            )
        row_sums = row_sums + contract(
            jnp.concatenate(left, axis=1), jnp.concatenate(right, axis=0), ((1,), (0,))
        )

    cols_t = col_ref[...]
    cum_grad = row_sums.T - step_t * cols_t
    later = contract(cum_grad, after, ((1,), (0,)), EXACT)
    step_grad = cols_t - rate * later
    raw_grad = step_grad / (1.0 + jnp.exp(-raw))
    out_ref[:STATE, :] = contract(query_t, score_grad, ((1,), (0,)), EXACT)
    query_all = (query_grad[:, :STATE] + query_grad[:, STATE:]).T
    out_ref[STATE : 2 * STATE, :] = query_all + contract(key_t, score_grad, ((1,), (1,)), EXACT)
    out_ref[2 * STATE :, :] = raw_grad
    if shards == 1:
        grad_ref[...] = out_ref[...].astype(jnp.bfloat16)
        send_ref[...] = jnp.zeros_like(send_ref)
        return
    for core in range(2):
        of_core = [
            out_ref[f * per : (f + 1) * per, :] for f in range(core, shards, 2)
        ]
        of_core = jnp.concatenate(of_core, axis=0).astype(jnp.bfloat16)
        for r in range(replicas):
            send_ref[2 * r + core] = of_core
    for at, k in enumerate(order):
        proj_ref[at * per : (at + 1) * per, :] = out_ref[shard_rows(where_ref, k, per), :]
    grad_ref[...] = proj_ref[...].astype(jnp.bfloat16)


def ssd_backward(where, rows_in, step_bias, decay_log, cross, enter, weights, order, replicas):
    block = rows_in.shape[0]
    heads = step_bias.shape[0]
    cols = sum(w.shape[0] for w in weights)
    apart = (2 * replicas, cols // 2, block) if len(order) > 1 else (16, 128)
    return pl.pallas_call(
        functools.partial(ssd_kernel, order, replicas),
        in_specs=[pl.BlockSpec(memory_space=pltpu.SMEM)] + whole_vmem(5 + len(order)),
        out_specs=whole_vmem(2),
        out_shape=[
            jax.ShapeDtypeStruct((cols, block), jnp.bfloat16),
            jax.ShapeDtypeStruct(apart, jnp.bfloat16),
        ],
        scratch_shapes=[
            pltpu.VMEM((cols, block), jnp.float32),
            pltpu.VMEM((heads, block), jnp.float32),
            pltpu.VMEM((cols, block), jnp.float32),
        ],
        compiler_params=params(),
        cost_estimate=pl.CostEstimate(
            flops=2 * block * cols * rows_in.shape[1],
            bytes_accessed=16 * rows_in.size,
            transcendentals=heads * block * block,
        ),
        name="ssd_backward",
    )(where, rows_in, step_bias.reshape(1, -1), decay_log.reshape(1, -1), cross, enter, *weights)


def block_grad_kernel(grad_ref, *refs):
    out_ref = refs[-1]
    weights = stacked(refs[:-1])
    out_ref[...] = contract(grad_ref[...].T, weights, ((1,), (0,))).astype(out_ref.dtype)


def block_gradient(grad, weights):
    depth = weights[0].shape[1]
    cols, block = grad.shape
    return pl.pallas_call(
        block_grad_kernel,
        in_specs=whole_vmem(1 + len(weights)),
        out_specs=pl.BlockSpec(memory_space=pltpu.VMEM),
        out_shape=jax.ShapeDtypeStruct((block, depth), jnp.bfloat16),
        compiler_params=params(),
        cost_estimate=pl.CostEstimate(
            flops=2 * block * cols * depth, bytes_accessed=4 * cols * depth, transcendentals=0
        ),
        name="block_gradient",
    )(grad, *weights)


def pieces_kernel(where_ref, rows_ref, own_ref, *outs):
    block = rows_ref.shape[0]
    width = outs[0].shape[1]
    for k, out in enumerate(outs):
        cols = pl.ds(pl.multiple_of((where_ref[0] ^ k) * width, 128), width)
        out[:block, :] = rows_ref[:, cols]
        out[block:, :] = own_ref[:, cols]


def column_pieces(where, rows_in, own, replicas):
    tokens, depth = rows_in.shape
    shape = (tokens + own.shape[0], depth // replicas)
    return pl.pallas_call(
        pieces_kernel,
        in_specs=[pl.BlockSpec(memory_space=pltpu.SMEM)] + whole_vmem(2),
        out_specs=whole_vmem(replicas),
        out_shape=[jax.ShapeDtypeStruct(shape, jnp.bfloat16)] * replicas,
        compiler_params=params(),
        name="column_pieces",
    )(where, rows_in, own)


def slice_kernel(replicas, where_ref, grads_ref, *refs):
    pieces, twin, out_ref = refs[:replicas], refs[replicas], refs[-1]
    tokens = twin.shape[0] // replicas
    core = where_ref[1] % 2
    left, right = [], []
    for other in range(2):
        for k in range(replicas):
            left.append(grads_ref[(where_ref[0] ^ k) * 2 + (core ^ other)])
            right.append(
                twin[k * tokens : (k + 1) * tokens, :] if other else pieces[k][:tokens, :]
            )
    total = contract(jnp.concatenate(left, axis=1), jnp.concatenate(right, axis=0), ((1,), (0,)))
    per = out_ref.shape[1]
    for z in range(out_ref.shape[0]):
        out_ref[z] = total[z * per : (z + 1) * per].astype(jnp.bfloat16)


def gradient_slice(where, grads, pieces, twin, chips):
    rows = grads.shape[1] // chips
    width = twin.shape[1]
    return pl.pallas_call(
        functools.partial(slice_kernel, len(pieces)),
        in_specs=[pl.BlockSpec(memory_space=pltpu.SMEM)] + whole_vmem(2 + len(pieces)),
        out_specs=pl.BlockSpec(memory_space=pltpu.VMEM),
        out_shape=jax.ShapeDtypeStruct((chips, rows, width), jnp.bfloat16),
        compiler_params=params(),
        name="gradient_slice",
    )(where, grads, *pieces, twin)


def stepped_kernel(sums_ref, *refs):
    pieces, out_ref = refs[:-1], refs[-1]
    replicas = len(pieces)
    rows = out_ref.shape[1]
    total = sums_ref[0].astype(jnp.float32)
    for z in range(1, sums_ref.shape[0]):
        total = total + sums_ref[z].astype(jnp.float32)
    level = pieces[0][-rows:, :].astype(jnp.float32)
    for piece in pieces[1:]:
        level = level + piece[-rows:, :].astype(jnp.float32)
    mean = ((level - inner_rate * total) * (1.0 / replicas)).astype(jnp.bfloat16)
    for r in range(replicas):
        out_ref[r] = mean


def stepped_slice(sums, pieces):
    _, rows, width = sums.shape
    return pl.pallas_call(
        stepped_kernel,
        in_specs=whole_vmem(1 + len(pieces)),
        out_specs=pl.BlockSpec(memory_space=pltpu.VMEM),
        out_shape=jax.ShapeDtypeStruct((len(pieces), rows, width), jnp.bfloat16),
        compiler_params=params(),
        name="stepped_slice",
    )(sums, *pieces)


def outer_kernel(stepped_ref, par_ref, mom_ref, new_par, new_mom):
    replicas, _, width = stepped_ref.shape
    for r in range(replicas):
        cols = slice(r * width, (r + 1) * width)
        old = par_ref[:, cols]
        pseudo = old - stepped_ref[r].astype(jnp.float32)
        fresh = momentum_decay * mom_ref[:, cols] + pseudo
        new_mom[:, cols] = fresh
        new_par[:, cols] = old - outer_rate * (pseudo + momentum_decay * fresh)


def outer_step(stepped, global_params, momentum):
    return pl.pallas_call(
        outer_kernel,
        in_specs=whole_vmem(3),
        out_specs=whole_vmem(2),
        out_shape=[jax.ShapeDtypeStruct(global_params.shape, jnp.float32)] * 2,
        compiler_params=params(),
        name="outer_step",
    )(stepped, global_params, momentum)


def on_device(
    sizes,
    block_input,
    ssd_input,
    out_grad,
    start_state,
    step_bias,
    decay_log,
    local_params,
    global_params,
    momentum,
):
    replicas, chips, cores = sizes
    local_rows = local_params[0]
    rows, depth = local_rows.shape
    own = local_rows.astype(jnp.bfloat16)
    seq_width = ssd_input.shape[1]
    blocks = start_state.shape[0]
    block = block_input.shape[0] // blocks
    fast = (
        cores == 2
        and chips == 4
        and rows % 8 == 0
        and replicas & (replicas - 1) == 0
        and depth % (128 * replicas) == 0
    )
    rep = lax.axis_index("rep")
    spot = lax.axis_index("line") * cores + lax.axis_index("core")
    where = jnp.stack([rep, spot]).astype(jnp.int32)

    def send(value, axis, k):
        count = dict(rep=replicas, line=chips, core=cores)[axis]
        return lax.ppermute(value, axis, [(i, i ^ k) for i in range(count)])

    if fast:
        near = send(own, "line", 1)
        far = send(own, "line", 3)
        middle = send(far, "line", 1)
        by_line = [own, near, far, middle]
        weights = by_line + [send(w, "core", 1) for w in by_line]
        order = (0, 2, 6, 4, 1, 3, 7, 5)
    else:
        weights = [lax.all_gather(own, ("line", "core"), axis=0, tiled=True)]
        order = (0,)

    grads, sends = [], []
    for b in range(blocks):
        seq = slice(b * block, (b + 1) * block)
        cross, enter = early_products(
            out_grad[seq], ssd_input[seq], start_state[b].reshape(seq_width, STATE)
        )
        grad, apart = ssd_backward(
            where, block_input[seq], step_bias, decay_log, cross, enter, weights, order, replicas
        )
        grads.append(grad)
        sends.append(apart)
    grad = grads[0] if blocks == 1 else jnp.concatenate(grads, axis=1)
    block_grad = block_gradient(grad, weights)

    if not fast:
        gradient = lax.psum_scatter(
            contract(grad, block_input, ((1,), (0,))),
            ("line", "core"),
            scatter_dimension=0,
            tiled=True,
        )
        pseudo = global_params - (local_rows - inner_rate * gradient)
        mean_pseudo = lax.psum(pseudo.astype(jnp.bfloat16), "rep").astype(jnp.float32) / replicas
        new_momentum = momentum_decay * momentum + mean_pseudo
        new_params = global_params - outer_rate * (mean_pseudo + momentum_decay * new_momentum)
        return (block_grad, new_params, new_momentum)

    apart = sends[0] if blocks == 1 else jnp.concatenate(sends, axis=2)
    tokens = blocks * block
    pieces = column_pieces(where, block_input, own, replicas)
    pieces = [pieces[0]] + [send(pieces[k], "rep", k) for k in range(1, replicas)]
    twin = send(jnp.concatenate([p[:tokens] for p in pieces], axis=0), "core", 1)

    def swap(value, axes):
        return lax.all_to_all(value, axes, split_axis=0, concat_axis=0, tiled=True)

    sums = gradient_slice(where, swap(apart, ("rep", "core")), pieces, twin, chips)
    stepped = stepped_slice(swap(sums, "line"), pieces)
    new_params, new_momentum = outer_step(swap(stepped, "rep"), global_params, momentum)
    return (block_grad, new_params, new_momentum)


def solution(mesh):
    replicas, shards = mesh.shape["rep"], mesh.shape["fsdp"]
    cores = 2 if shards % 2 == 0 else 1
    sizes = (replicas, shards // cores, cores)
    apart = jax.sharding.Mesh(mesh.devices.reshape(sizes), ("rep", "line", "core"))
    fsdp = ("line", "core")
    rows = P(("rep", "line", "core"), None)
    placed = (
        rows,
        rows,
        rows,
        P(("rep", "line", "core"), None, None),
        P(),
        P(),
        P("rep", fsdp, None),
        P(fsdp, None),
        P(fsdp, None),
    )
    return jax.shard_map(
        functools.partial(on_device, sizes),
        mesh=apart,
        in_specs=placed,
        out_specs=(rows, P(fsdp, None), P(fsdp, None)),
        check_vma=False,
    )
```

time: 102 us -> 90.4 us (0.89)
  starting transfers between devices: 38 us -> 15.6 us
  blocking collectives: 0 us -> 20.3 us
  local copies, waits for them, and re-layouts: 12.4 us -> 5.81 us
  between operations: 5.69 us -> 0.77 us
  Pallas kernels: 16.5 us -> 18.7 us
  waiting for transfers between devices: 24.6 us -> 26.5 us
  matrix products: 1.43 us -> 0 us
  other arithmetic: 3.34 us -> 2.14 us
    ppermute x34 -> x11, starting transfers between devices: 38 us -> 12.3 us  [send(): return lax.ppermute(value, axis, [(i, i ^ k) for i in range(count)])]
    all_to_all x0 -> x2, blocking collectives: none -> 20.3 us  [swap(): return lax.all_to_all(value, axes, split_axis=0, concat_axis=0, tiled=True)]
    another operation x2 -> x0, local copies, waits for them, and re-layouts: 4.52 us -> none  [the longest x1 4.43 us: on_device(): owners = jnp.stack(owners).astype(jnp.int32)]
    all_to_all x0 -> x1, starting transfers between devices: none -> 3.37 us  [swap(): return lax.all_to_all(value, axes, split_axis=0, concat_axis=0, tiled=True)]
    reshape x2 -> x0, local copies, waits for them, and re-layouts: 2.72 us -> none  [the longest x1 1.36 us: ssd_backward(): step_bias.reshape(-1, 1)]
    unnamed x24 -> x16, local copies, waits for them, and re-layouts: 1.05 us -> 3.69 us
    all_to_all x0 -> x1, waiting for transfers between devices: none -> 2.33 us  [swap(): return lax.all_to_all(value, axes, split_axis=0, concat_axis=0, tiled=True)]
    pallas_call x4 -> x6, Pallas kernels: 11.6 us -> 13.9 us  [the longest x1 6.99 us: ssd_backward(): pl.pallas_call(functools.partial(ssd_kernel, order, replicas), in_specs=[...]
  transfers between devices with their start and end apart: 34 -> 12, of which waited for: 11 -> 6; matrix products, arithmetic and copies ran while one was open for 15% -> 2% of each run, Pallas kernels for 13% -> 16%
where the time goes in v2:
time: 90.4 us; the launch traced here: 89.8 us
  waiting for transfers between devices  26.5 us (29%)
  blocking collectives  20.3 us (22%)
  Pallas kernels  18.7 us (21%)
  starting transfers between devices  15.6 us (17%)
  local copies, waits for them, and re-layouts  5.81 us (6%)
  other arithmetic  2.14 us (2%)
    ppermute x11, waiting for transfers between devices, send(): return lax.ppermute(value, axis, [(i, i ^ k) for i in range(count)])  24.2 us
    all_to_all x2, blocking collectives, swap(): return lax.all_to_all(value, axes, split_axis=0, concat_axis=0, tiled=True)  20.3 us
    ppermute x11, starting transfers between devices, send(): return lax.ppermute(value, axis, [(i, i ^ k) for i in range(count)])  12.3 us
    pallas_call x1, Pallas kernels, ssd_backward(): pl.pallas_call(functools.partial(ssd_kernel, order, replicas), in_specs=[...  6.99 us
    pallas_call x1, Pallas kernels, early_products(): pl.pallas_call(early_kernel, grid=(steps,), in_specs=[pl.BlockSpec((block...  4.79 us
    unnamed x16, local copies, waits for them, and re-layouts  3.69 us
    all_to_all x1, starting transfers between devices, swap(): return lax.all_to_all(value, axes, split_axis=0, concat_axis=0, tiled=True)  3.37 us
    pallas_call x1, Pallas kernels, block_gradient(): pl.pallas_call(block_grad_kernel, in_specs=whole_vmem(1 + len(weights)),...  2.83 us
  transfers between devices with their start and end apart: 12, of which 6 were waited for; matrix products, arithmetic and copies ran while one was open for 2% of the time, Pallas kernels for 16%

profile of v2, /device:TPU:0, one launch (start us, length us, event | category | flops | bytes accessed | tf_op | source)
XLA Modules:
  0.0 89.8 jit_solution(7385922294399119772)
XLA Ops:
  0.6 1.0 %convert_bitcast_fusion.rest_0_.refs_0_.own_ref = bf16[24,4096]{1,0:T(8,128)(2,1)S(1)} fusion(f32[1,24,4096]{2,1,0:T(8,128)} %param.15), kind=kLoop, calls=%fused_computation.1 | loop fusion | flops 98304 | bytes 589824 | tf_op jit(solution)/shard_map/convert_element_type | solution.py:350
  1.7 0.1 pad_add_fusion.where_ref
  1.7 1.2 %copy-done = bf16[128,4096]{1,0:T(8,128)(2,1)S(1)} copy-done((bf16[128,4096]{1,0:T(8,128)(2,1)S(1)}, bf16[128,4096]{1,0:T(8,128)(2,1)}, u32[]{:S(2)}) %copy-start) | copy-done | bytes 1048600
  3.0 0.6 column_pieces.1
  3.6 4.0 %collective-permute-start.9 = (bf16[152,1024]{1,0:T(8,128)(2,1)S(1)}, bf16[152,1024]{1,0:T(8,128)(2,1)S(1)}, u32[]{:S(2)}, u32[]{:S(2)}) collective-permute-start(bf16[152,1024]{1,0:T(8,128)(2,1)S(1)} %get-tuple-element.20), channel_id=1, source_target_pairs={{0,24},{8,16},{16,8},{24,0},{1,25},{9,17},{17,9},{25,1},{2,26},{10... | collective-permute-start | bytes 933896 | tf_op jit(solution)/shard_map/ppermute | solution.py:367
  7.6 0.5 collective-permute-start.8
  8.1 0.1 collective-permute-start.7
  8.2 7.6 %collective-permute-done.9.refs_3_ = bf16[152,1024]{1,0:T(8,128)(2,1)S(1)} collective-permute-done((bf16[152,1024]{1,0:T(8,128)(2,1)S(1)}, bf16[152,1024]{1,0:T(8,128)(2,1)S(1)}, u32[]{:S(2)}, u32[]{:S(2)}) %collective-permute-start.9) | collective-permute-done | bytes 311328 | tf_op jit(solution)/shard_map/ppermute | solution.py:367
  15.8 5.8 %collective-permute-done.8.refs_2_ = bf16[152,1024]{1,0:T(8,128)(2,1)S(1)} collective-permute-done((bf16[152,1024]{1,0:T(8,128)(2,1)S(1)}, bf16[152,1024]{1,0:T(8,128)(2,1)S(1)}, u32[]{:S(2)}, u32[]{:S(2)}) %collective-permute-start.8) | collective-permute-done | bytes 311328 | tf_op jit(solution)/shard_map/ppermute | solution.py:367
  21.6 0.3 collective-permute-done.7.refs_1_
  21.9 1.0 %pad_maximum_fusion = bf16[512,1024]{1,0:T(8,128)(2,1)} fusion(bf16[128,1024]{1,0:T(8,128)(2,1)S(1)} %slice.18, bf16[128,1024]{1,0:T(8,128)(2,1)S(1)} %slice.17, bf16[128,1024]{1,0:T(8,128)(2,1)S(1)} %slice.16, bf16[128,1024]{1,0:T(8,128)(2,1)S(1)} %slice.12), kind=kLoop, calls=%fused_computation | loop fusion | flops 4194304 | bytes 2097152 | tf_op jit(solution)/shard_map/concatenate | solution.py:411
  23.0 0.0 collective-permute-start.10
  23.0 3.7 %collective-permute-start.1 = (bf16[24,4096]{1,0:T(8,128)(2,1)S(1)}, bf16[24,4096]{1,0:T(8,128)(2,1)}, u32[]{:S(2)}, u32[]{:S(2)}) collective-permute-start(bf16[24,4096]{1,0:T(8,128)(2,1)S(1)} %convert_bitcast_fusion.rest_0_.refs_0_.own_ref), channel_id=1, source_target_pairs={{0,6},{2,4},{4,2},{6,0},{1,7},{3,5},{5,3},{7,1},{8,14},{10,12},{12... | collective-permute-start | bytes 589832 | tf_op jit(solution)/shard_map/ppermute | solution.py:367
  26.6 6.0 %collective-permute-done.1.rest_2_.refs_2_ = bf16[24,4096]{1,0:T(8,128)(2,1)} collective-permute-done((bf16[24,4096]{1,0:T(8,128)(2,1)S(1)}, bf16[24,4096]{1,0:T(8,128)(2,1)}, u32[]{:S(2)}, u32[]{:S(2)}) %collective-permute-start.1) | collective-permute-done | bytes 196640 | tf_op jit(solution)/shard_map/ppermute | solution.py:367
  32.7 3.5 %collective-permute-start.2 = (bf16[24,4096]{1,0:T(8,128)(2,1)}, bf16[24,4096]{1,0:T(8,128)(2,1)}, u32[]{:S(2)}, u32[]{:S(2)}) collective-permute-start(bf16[24,4096]{1,0:T(8,128)(2,1)} %collective-permute-done.1.rest_2_.refs_2_), channel_id=1, source_target_pairs={{0,2},{2,0},{4,6},{6,4},{1,3},{3,1},{5,7},{7,5},{8,10},{10,8},{12,... | collective-permute-start | bytes 589832 | tf_op jit(solution)/shard_map/ppermute | solution.py:367
  36.2 0.5 collective-permute-start.5
  36.7 0.0 collective-permute-start.4
  36.7 4.5 %collective-permute-done.2.rest_3_.refs_3_ = bf16[24,4096]{1,0:T(8,128)(2,1)} collective-permute-done((bf16[24,4096]{1,0:T(8,128)(2,1)}, bf16[24,4096]{1,0:T(8,128)(2,1)}, u32[]{:S(2)}, u32[]{:S(2)}) %collective-permute-start.2) | collective-permute-done | bytes 196640 | tf_op jit(solution)/shard_map/ppermute | solution.py:367
  41.2 2.1 %reshape_squeeze.3.state_ref = bf16[4096,64]{1,0:T(8,128)(2,1)S(1)} reshape(bf16[1,64,4096]{2,1,0:T(8,128)(2,1)} %param.12) | data formatting | bytes 1048576 | tf_op jit(solution)/shard_map/reshape;squeeze | solution.py:384
  43.3 0.0 copy-start.2
  43.3 1.2 %copy-done.2 = bf16[128,4096]{1,0:T(8,128)(2,1)S(1)} copy-done((bf16[128,4096]{1,0:T(8,128)(2,1)S(1)}, bf16[128,4096]{1,0:T(8,128)(2,1)}, u32[]{:S(2)}) %copy-start.2) | copy-done | bytes 1048600
  44.5 1.2 %copy-done.3 = bf16[128,4096]{1,0:T(8,128)(2,1)S(1)} copy-done((bf16[128,4096]{1,0:T(8,128)(2,1)S(1)}, bf16[128,4096]{1,0:T(8,128)(2,1)}, u32[]{:S(2)}) %copy-start.3) | copy-done | bytes 1048600
  45.7 4.8 %early_products.1 = (bf16[64,128,128]{2,1,0:T(8,128)(2,1)S(1)}, f32[128,4096]{1,0:T(8,128)}) custom-call(bf16[128,4096]{1,0:T(8,128)(2,1)S(1)} %copy-done.2, bf16[128,4096]{1,0:T(8,128)(2,1)S(1)} %copy-done.3, bf16[4096,64]{1,0:T(8,128)(2,1)S(1)} %reshape_squeeze.3.state_ref), custom_call_target="tpu_custom_call" | custom-call | flops 536870912 | bytes 4194304 | tf_op jit(solution)/shard_map/early_products/pallas_call | solution.py:66
  50.6 7.0 %ssd_backward.1 = (bf16[192,128]{1,0:T(8,128)(2,1)S(1)}, bf16[8,96,128]{2,1,0:T(8,128)(2,1)S(1)}) custom-call(s32[2]{0:T(128)S(1)} %pad_add_fusion.where_ref, bf16[128,4096]{1,0:T(8,128)(2,1)S(1)} %copy-done.1, f32[1,64]{1,0:T(1,128)S(1)} %bitcast.6, f32[1,64]{1,0:T(1,128)S(1)} %bitcast.7, bf16[64,128,128]{2,1,0:T(8,128)(2,1)S(1)} %get-tuple-element.13.cross_ref, ...), custom_call_target="tpu_custom_call" | custom-call | flops 201326592 | bytes 8388608 | tf_op jit(solution)/shard_map/ssd_backward/pallas_call | solution.py:189
  57.6 9.1 %all_to_all.15.grads_ref = bf16[8,96,128]{2,1,0:T(8,128)(2,1)S(1)} all-to-all(bf16[8,96,128]{2,1,0:T(8,128)(2,1)S(1)} %get-tuple-element.16), channel_id=1, replica_groups=mesh['rep'=4,'line'=4,'core'=2] {'rep','core'}, dimensions={0} | all-to-all | bytes 393216 | tf_op jit(solution)/shard_map/all_to_all | solution.py:414
  66.7 1.7 %gradient_slice.1 = bf16[4,24,1024]{2,1,0:T(8,128)(2,1)S(1)} custom-call(s32[2]{0:T(128)S(1)} %pad_add_fusion.where_ref, bf16[8,96,128]{2,1,0:T(8,128)(2,1)S(1)} %all_to_all.15.grads_ref, bf16[152,1024]{1,0:T(8,128)(2,1)S(1)} %get-tuple-element.17.refs_0_, bf16[152,1024]{1,0:T(8,128)(2,1)S(1)} %collective-permute-done.7.refs_1_, ...), custom_call_target="tpu_custom_call" | custom-call | tf_op jit(solution)/shard_map/gradient_slice/pallas_call | solution.py:276
  68.4 11.2 %all_to_all.16.sums_ref = bf16[4,24,1024]{2,1,0:T(8,128)(2,1)S(1)} all-to-all(bf16[4,24,1024]{2,1,0:T(8,128)(2,1)S(1)} %gradient_slice.1), channel_id=1, replica_groups=mesh['rep'=4,'line'=4,'core'=2] {'line'}, dimensions={0} | all-to-all | bytes 393216 | tf_op jit(solution)/shard_map/all_to_all | solution.py:414
  79.6 0.7 stepped_slice.1
  80.3 3.4 %all-to-all-start.2 = ((bf16[4,24,1024]{2,1,0:T(8,128)(2,1)}), bf16[4,24,1024]{2,1,0:T(8,128)(2,1)S(1)}, u32[]{:S(2)}, u32[]{:S(2)}) async-start(bf16[4,24,1024]{2,1,0:T(8,128)(2,1)} %stepped_slice.1), calls=%async_computation.2 | async-start | bytes 393216 | tf_op jit(solution)/shard_map/all_to_all | solution.py:414
  83.7 2.8 %block_gradient.1 = bf16[128,4096]{1,0:T(8,128)(2,1)} custom-call(bf16[192,128]{1,0:T(8,128)(2,1)S(1)} %get-tuple-element.15.grad_ref, bf16[24,4096]{1,0:T(8,128)(2,1)S(1)} %convert_bitcast_fusion.rest_0_.refs_0_.own_ref, bf16[24,4096]{1,0:T(8,128)(2,1)} %collective-permute-done.rest_1_.refs_1_, bf16[24,4096]{1,0:T(8,128)(2,1)} %collective-permute-done.1.rest_2_.refs_2_, ...), custom_call_target="tpu_custom_call" | custom-call | flops 201326592 | bytes 3145728 | tf_op jit(solution)/shard_map/block_gradient/pallas_call | solution.py:221
  86.5 2.3 %all-to-all-done.2.stepped_ref = bf16[4,24,1024]{2,1,0:T(8,128)(2,1)S(1)} async-done(((bf16[4,24,1024]{2,1,0:T(8,128)(2,1)}), bf16[4,24,1024]{2,1,0:T(8,128)(2,1)S(1)}, u32[]{:S(2)}, u32[]{:S(2)}) %all-to-all-start.2) | async-done | bytes 196640 | tf_op jit(solution)/shard_map/all_to_all | solution.py:414
  88.8 1.0 %outer_step.1 = (f32[24,4096]{1,0:T(8,128)}, f32[24,4096]{1,0:T(8,128)}) custom-call(bf16[4,24,1024]{2,1,0:T(8,128)(2,1)S(1)} %all-to-all-done.2.stepped_ref, f32[24,4096]{1,0:T(8,128)S(1)} %copy-done.4, f32[24,4096]{1,0:T(8,128)S(1)} %copy-done.5), custom_call_target="tpu_custom_call" | custom-call | tf_op jit(solution)/shard_map/outer_step/pallas_call | solution.py:325
  (25 shorter events, 0.1 us)
Async XLA Ops:
  1.7 1.2 %copy-start = (bf16[128,4096]{1,0:T(8,128)(2,1)S(1)}, bf16[128,4096]{1,0:T(8,128)(2,1)}, u32[]{:S(2)}) copy-start(bf16[128,4096]{1,0:T(8,128)(2,1)} %rows_ref.3) | copy-start | bytes 3145732
  3.6 12.2 %collective-permute-start.9 = (bf16[152,1024]{1,0:T(8,128)(2,1)S(1)}, bf16[152,1024]{1,0:T(8,128)(2,1)S(1)}, u32[]{:S(2)}, u32[]{:S(2)}) collective-permute-start(bf16[152,1024]{1,0:T(8,128)(2,1)S(1)} %get-tuple-element.20), channel_id=1, source_target_pairs={{0,24},{8,16},{16,8},{24,0},{1,25},{9,17},{17,9},{25,1},{2,26},{10... | collective-permute-start | bytes 933896 | tf_op jit(solution)/shard_map/ppermute | solution.py:367
  7.6 14.0 %collective-permute-start.8 = (bf16[152,1024]{1,0:T(8,128)(2,1)S(1)}, bf16[152,1024]{1,0:T(8,128)(2,1)S(1)}, u32[]{:S(2)}, u32[]{:S(2)}) collective-permute-start(bf16[152,1024]{1,0:T(8,128)(2,1)S(1)} %get-tuple-element.19), channel_id=1, source_target_pairs={{0,16},{8,24},{16,0},{24,8},{1,17},{9,25},{17,1},{25,9},{2,18},{10... | collective-permute-start | bytes 933896 | tf_op jit(solution)/shard_map/ppermute | solution.py:367
  8.1 13.8 %collective-permute-start.7 = (bf16[152,1024]{1,0:T(8,128)(2,1)S(1)}, bf16[152,1024]{1,0:T(8,128)(2,1)S(1)}, u32[]{:S(2)}, u32[]{:S(2)}) collective-permute-start(bf16[152,1024]{1,0:T(8,128)(2,1)S(1)} %get-tuple-element.18), channel_id=1, source_target_pairs={{0,8},{8,0},{16,24},{24,16},{1,9},{9,1},{17,25},{25,17},{2,10},{10... | collective-permute-start | bytes 933896 | tf_op jit(solution)/shard_map/ppermute | solution.py:367
  22.9 27.6 %copy-start.1 = (bf16[128,4096]{1,0:T(8,128)(2,1)S(1)}, bf16[128,4096]{1,0:T(8,128)(2,1)}, u32[]{:S(2)}) copy-start(bf16[128,4096]{1,0:T(8,128)(2,1)} %rows_ref.3) | copy-start | bytes 3145732
  22.9 27.6 %copy-start.6 = (f32[64]{0:T(128)S(1)}, f32[64]{0:T(128)}, u32[]{:S(2)}) copy-start(f32[64]{0:T(128)} %param.13) | copy-start | bytes 772
  23.0 27.6 %copy-start.7 = (f32[64]{0:T(128)S(1)}, f32[64]{0:T(128)}, u32[]{:S(2)}) copy-start(f32[64]{0:T(128)} %param.14) | copy-start | bytes 772
  23.0 43.7 %collective-permute-start.10 = (bf16[512,1024]{1,0:T(8,128)(2,1)}, bf16[512,1024]{1,0:T(8,128)(2,1)}, u32[]{:S(2)}, u32[]{:S(2)}) collective-permute-start(bf16[512,1024]{1,0:T(8,128)(2,1)} %pad_maximum_fusion), channel_id=1, source_target_pairs={{0,1},{1,0},{2,3},{3,2},{4,5},{5,4},{6,7},{7,6},{8,9},{9,8},{10,11... | collective-permute-start | bytes 3145736 | tf_op jit(solution)/shard_map/ppermute | solution.py:367
  23.0 9.7 %collective-permute-start.1 = (bf16[24,4096]{1,0:T(8,128)(2,1)S(1)}, bf16[24,4096]{1,0:T(8,128)(2,1)}, u32[]{:S(2)}, u32[]{:S(2)}) collective-permute-start(bf16[24,4096]{1,0:T(8,128)(2,1)S(1)} %convert_bitcast_fusion.rest_0_.refs_0_.own_ref), channel_id=1, source_target_pairs={{0,6},{2,4},{4,2},{6,0},{1,7},{3,5},{5,3},{7,1},{8,14},{10,12},{12... | collective-permute-start | bytes 589832 | tf_op jit(solution)/shard_map/ppermute | solution.py:367
  26.6 10.0 %collective-permute-start = (bf16[24,4096]{1,0:T(8,128)(2,1)S(1)}, bf16[24,4096]{1,0:T(8,128)(2,1)}, u32[]{:S(2)}, u32[]{:S(2)}) collective-permute-start(bf16[24,4096]{1,0:T(8,128)(2,1)S(1)} %convert_bitcast_fusion.rest_0_.refs_0_.own_ref), channel_id=1, source_target_pairs={{0,2},{2,0},{4,6},{6,4},{1,3},{3,1},{5,7},{7,5},{8,10},{10,8},{12,... | collective-permute-start | bytes 589832 | tf_op jit(solution)/shard_map/ppermute | solution.py:367
  32.7 8.5 %collective-permute-start.2 = (bf16[24,4096]{1,0:T(8,128)(2,1)}, bf16[24,4096]{1,0:T(8,128)(2,1)}, u32[]{:S(2)}, u32[]{:S(2)}) collective-permute-start(bf16[24,4096]{1,0:T(8,128)(2,1)} %collective-permute-done.1.rest_2_.refs_2_), channel_id=1, source_target_pairs={{0,2},{2,0},{4,6},{6,4},{1,3},{3,1},{5,7},{7,5},{8,10},{10,8},{12,... | collective-permute-start | bytes 589832 | tf_op jit(solution)/shard_map/ppermute | solution.py:367
  36.2 14.3 %collective-permute-start.3 = (bf16[24,4096]{1,0:T(8,128)(2,1)S(1)}, bf16[24,4096]{1,0:T(8,128)(2,1)}, u32[]{:S(2)}, u32[]{:S(2)}) collective-permute-start(bf16[24,4096]{1,0:T(8,128)(2,1)S(1)} %convert_bitcast_fusion.rest_0_.refs_0_.own_ref), channel_id=1, source_target_pairs={{0,1},{1,0},{2,3},{3,2},{4,5},{5,4},{6,7},{7,6},{8,9},{9,8},{10,11... | collective-permute-start | bytes 589832 | tf_op jit(solution)/shard_map/ppermute | solution.py:367
  36.2 14.3 %collective-permute-start.5 = (bf16[24,4096]{1,0:T(8,128)(2,1)}, bf16[24,4096]{1,0:T(8,128)(2,1)}, u32[]{:S(2)}, u32[]{:S(2)}) collective-permute-start(bf16[24,4096]{1,0:T(8,128)(2,1)} %collective-permute-done.1.rest_2_.refs_2_), channel_id=1, source_target_pairs={{0,1},{1,0},{2,3},{3,2},{4,5},{5,4},{6,7},{7,6},{8,9},{9,8},{10,11... | collective-permute-start | bytes 589832 | tf_op jit(solution)/shard_map/ppermute | solution.py:367
  36.7 13.8 %collective-permute-start.4 = (bf16[24,4096]{1,0:T(8,128)(2,1)}, bf16[24,4096]{1,0:T(8,128)(2,1)}, u32[]{:S(2)}, u32[]{:S(2)}) collective-permute-start(bf16[24,4096]{1,0:T(8,128)(2,1)} %collective-permute-done.rest_1_.refs_1_), channel_id=1, source_target_pairs={{0,1},{1,0},{2,3},{3,2},{4,5},{5,4},{6,7},{7,6},{8,9},{9,8},{10,11... | collective-permute-start | bytes 589832 | tf_op jit(solution)/shard_map/ppermute | solution.py:367
  41.2 9.3 %collective-permute-start.6 = (bf16[24,4096]{1,0:T(8,128)(2,1)}, bf16[24,4096]{1,0:T(8,128)(2,1)}, u32[]{:S(2)}, u32[]{:S(2)}) collective-permute-start(bf16[24,4096]{1,0:T(8,128)(2,1)} %collective-permute-done.2.rest_3_.refs_3_), channel_id=1, source_target_pairs={{0,1},{1,0},{2,3},{3,2},{4,5},{5,4},{6,7},{7,6},{8,9},{9,8},{10,11... | collective-permute-start | bytes 589832 | tf_op jit(solution)/shard_map/ppermute | solution.py:367
  43.3 1.2 %copy-start.2 = (bf16[128,4096]{1,0:T(8,128)(2,1)S(1)}, bf16[128,4096]{1,0:T(8,128)(2,1)}, u32[]{:S(2)}) copy-start(bf16[128,4096]{1,0:T(8,128)(2,1)} %cot_ref.1) | copy-start | bytes 3145732
  44.5 1.2 %copy-start.3 = (bf16[128,4096]{1,0:T(8,128)(2,1)S(1)}, bf16[128,4096]{1,0:T(8,128)(2,1)}, u32[]{:S(2)}) copy-start(bf16[128,4096]{1,0:T(8,128)(2,1)} %val_ref.1) | copy-start | bytes 3145732
  79.6 9.3 %copy-start.4 = (f32[24,4096]{1,0:T(8,128)S(1)}, f32[24,4096]{1,0:T(8,128)}, u32[]{:S(2)}) copy-start(f32[24,4096]{1,0:T(8,128)} %par_ref.1) | copy-start | bytes 1179652
  79.6 9.3 %copy-start.5 = (f32[24,4096]{1,0:T(8,128)S(1)}, f32[24,4096]{1,0:T(8,128)}, u32[]{:S(2)}) copy-start(f32[24,4096]{1,0:T(8,128)} %mom_ref.1) | copy-start | bytes 1179652
  80.3 8.5 %all-to-all-start.2 = ((bf16[4,24,1024]{2,1,0:T(8,128)(2,1)}), bf16[4,24,1024]{2,1,0:T(8,128)(2,1)S(1)}, u32[]{:S(2)}, u32[]{:S(2)}) async-start(bf16[4,24,1024]{2,1,0:T(8,128)(2,1)} %stepped_slice.1), calls=%async_computation.2 | async-start | bytes 393216 | tf_op jit(solution)/shard_map/all_to_all | solution.py:414
